TPU v7x, 32 devices: a whole 2x2x4 slice. The times are simulated.
32 devices in a mesh: az: 8 (over z, x), ht: 4 (over y, core).
Axes of the slice: x: 2, y: 2, z: 4, core: 2. Of those that a mesh axis runs over, the one named last changes fastest.
Arguments:
- object_field: bfloat16 [256, 3, 2, 4096], P('ht', None, None, 'az'), may hold values from -6 to 6
- propagator: bfloat16 [3, 2, 256, 256], replicated, may hold values from -0.25 to 0.25
- kernel_taps: float32 [3, 2, 129], replicated, may hold values from -0.5 to 0.5
- band_reach: int32 [3], replicated, may hold values from 16 to 64, as said below
- sector_offset: int32 [8], replicated, may hold values from 0 to 511, as said below
- sector_width: int32 [8], replicated, may hold values from 768 to 1536
- target_index: int32 [8], replicated, may hold values from 0 to 3
- target_maps: float32 [4, 256, 3, 256], P(None, 'ht'), may hold values from 0 to 3
Outputs:
- object_grad: float32 [256, 3, 2, 4096], P('ht', None, None, 'az')
Inputs may be any that keep to these rules, and one draw needn't show every extreme that they name: One wavelength has band_reach 64, another 64 // 4. Sector s's window begins at azimuth s * 512 + sector_offset[s] and wraps around the cylinder.
All inputs are finite; a program needn't handle non-finite values.
Results may differ from a plain program's by a relative error of at most 0.0095.
Values may be sent and summed in bfloat16 or wider, within the bound.
A program may use at most 64 MiB of HBM per device.

v0:
```python
import math

import jax
import jax.numpy as jnp
from jax import lax
from jax.sharding import PartitionSpec as P

FREQS = 256
REACH = 64


def with_halo(x, sides, width):
    for axis, dim in sides:
        size, length = (lax.axis_size(axis), x.shape[dim])
        up = [(i, (i + 1) % size) for i in range(size)]
        down = [(j, i) for i, j in up]
        last = lax.slice_in_dim(x, length - width, length, axis=dim)
        initial = lax.slice_in_dim(x, 0, width, axis=dim)
        before = lax.ppermute(last, axis, up)
        after = lax.ppermute(initial, axis, down)
        x = jnp.concatenate([before, x, after], axis=dim)
    return x


def from_behind(block, axis, distance):
    devices = range(lax.axis_size(axis))
    route = [((i - distance) % len(devices), i) for i in devices]
    return lax.ppermute(block, axis, route)


def height_block(propagator):
    real_part = propagator[:, 0]
    imag_part = propagator[:, 1]
    upper = jnp.stack([real_part, -imag_part], axis=2)
    lower = jnp.stack([imag_part, real_part], axis=2)
    return jnp.stack([upper, lower], axis=1)


def masked(kernel_taps, band_reach):
    distance = jnp.abs(jnp.arange(2 * REACH + 1, dtype=jnp.int32) - REACH)
    keep = distance[None, :] <= band_reach[:, None]
    return jnp.where(keep[:, None, :], kernel_taps, jnp.zeros_like(kernel_taps))


def toeplitz(real_taps, imag_taps):
    block_size = 2 * REACH
    period = 3 * block_size
    wave_count = real_taps.shape[0]

    def arrange(tap_values):
        padded = jnp.concatenate(
            [tap_values, jnp.zeros((wave_count, period - block_size - 1), tap_values.dtype)], axis=1
        )
        tiled = jnp.tile(padded, (1, block_size))[:, : block_size * (period - 1)]
        return tiled.reshape(wave_count, block_size, period - 1)[:, :, : 2 * block_size]

    real_lay = arrange(real_taps)
    imag_lay = arrange(imag_taps)
    upper = jnp.stack([real_lay, imag_lay], axis=1)
    lower = jnp.stack([-imag_lay, real_lay], axis=1)
    return jnp.stack([upper, lower], axis=1).astype(jnp.bfloat16)


def convolve(extended, coupling):
    row_count, wave_count, part_count, full_length = extended.shape
    block_size = 2 * REACH
    block_count = full_length // block_size - 1
    shaped = extended.reshape(row_count, wave_count, part_count, block_count + 1, block_size)
    windows = jnp.concatenate([shaped[:, :, :, :-1], shaped[:, :, :, 1:]], axis=4)
    result = jnp.einsum("hwcbi,wcdji->hwdbj", windows, coupling, preferred_element_type=jnp.float32)
    return result.reshape(row_count, wave_count, part_count, block_count * block_size)


def spectrum_table(offset, span_width, az_count):
    places = jnp.arange(4 * az_count, dtype=jnp.int32) - offset
    inside = (places >= 0) & (places < span_width)
    places = jnp.where(inside, places, 0)
    frequency = jnp.arange(FREQS, dtype=jnp.int32)
    phases = jnp.mod(places[:, None] * frequency[None, :], FREQS).astype(jnp.float32) * (
        2.0 * math.pi / FREQS
    )
    span_float = span_width.astype(jnp.float32)
    taper = 0.5 - 0.5 * jnp.cos((places.astype(jnp.float32) + 0.5) * (2.0 * math.pi) / span_float)
    taper = jnp.where(inside, taper, 0.0) / jnp.sqrt(span_float)
    cosine = taper[:, None] * jnp.cos(phases)
    sine = taper[:, None] * jnp.sin(phases)
    upper = jnp.stack([cosine, -sine], axis=1)
    lower = jnp.stack([sine, cosine], axis=1)
    return jnp.stack([upper, lower], axis=0).astype(jnp.bfloat16)


def view_slopes(window, spectra_table, target_plane):
    spectrum = jnp.einsum(
        "hwcp,cpdk->hwdk", window, spectra_table, preferred_element_type=jnp.float32
    )
    power = spectrum[:, :, 0] * spectrum[:, :, 0] + spectrum[:, :, 1] * spectrum[:, :, 1]
    misfit = power - target_plane
    slope = (2.0 * misfit[:, :, None, :] * spectrum).astype(jnp.bfloat16)
    back = jnp.einsum("hwdk,cpdk->hwcp", slope, spectra_table, preferred_element_type=jnp.float32)
    return back.astype(jnp.bfloat16)


def on_device(
    object_field,
    propagator,
    kernel_taps,
    band_reach,
    sector_offset,
    sector_width,
    target_index,
    target_maps,
):
    row_count, wave_count, part_count, az_count = object_field.shape
    loop_size = lax.axis_size("az")
    first_row = lax.axis_index("ht") * row_count
    coupling = height_block(propagator)
    own_rows = lax.dynamic_slice_in_dim(coupling, first_row, row_count, 2)
    zero_field = jnp.zeros((row_count, wave_count, part_count, az_count), jnp.float32)
    columns = own_rows
    height_field = jnp.einsum(
        "wdhcg,gwca->hwda",
        columns,
        lax.all_gather(object_field, "ht", axis=0, tiled=True),
        preferred_element_type=jnp.float32,
    ).astype(jnp.bfloat16)
    masked_taps = masked(kernel_taps, band_reach)
    forward = toeplitz(masked_taps[:, 0], masked_taps[:, 1])
    backward = toeplitz(masked_taps[:, 0, ::-1], -masked_taps[:, 1, ::-1])
    extended = with_halo(height_field, (("az", 3),), REACH)
    hologram = convolve(extended, forward).astype(jnp.bfloat16)
    home_lead = 0
    sector = jnp.mod(lax.axis_index("az") - home_lead, loop_size)
    relatives = [position - home_lead for position in range(4)]
    blocks = []
    for relative in relatives:
        if relative == 0:
            blocks.append(hologram)
        else:
            blocks.append(from_behind(hologram, "az", -relative))
    window = jnp.concatenate(blocks, axis=3)
    offset = lax.dynamic_index_in_dim(sector_offset, sector, 0, False)
    span_width = lax.dynamic_index_in_dim(sector_width, sector, 0, False)
    pattern = lax.dynamic_index_in_dim(target_index, sector, 0, False)
    target_plane = lax.dynamic_index_in_dim(target_maps, pattern, 0, False)
    spectra_table = spectrum_table(offset, span_width, az_count)
    slopes = view_slopes(window, spectra_table, target_plane)
    summed = zero_field
    for position, relative in enumerate(relatives):
        portion = slopes[..., position * az_count : (position + 1) * az_count]
        if relative == 0:
            summed = portion.astype(jnp.float32)
        else:
            summed = summed + from_behind(portion, "az", relative).astype(jnp.float32)
    hologram_grad = summed.astype(jnp.bfloat16)
    grad_extended = with_halo(hologram_grad, (("az", 3),), REACH)
    field_grad = convolve(grad_extended, backward).astype(jnp.bfloat16)
    columns = own_rows
    return lax.psum_scatter(
        jnp.einsum(
            "wdhcg,hwda->gwca", columns, field_grad, preferred_element_type=jnp.float32
        ).astype(jnp.bfloat16),
        "ht",
        scatter_dimension=0,
        tiled=True,
    ).astype(jnp.float32)


def solution(mesh):
    in_specs = (P("ht", None, None, "az"), P(), P(), P(), P(), P(), P(), P(None, "ht", None, None))
    out_specs = P("ht", None, None, "az")
    return jax.shard_map(
        on_device, mesh=mesh, in_specs=in_specs, out_specs=out_specs, check_vma=False
    )
```

profile of v0, /device:TPU:0, one launch (start us, length us, event | category | flops | bytes accessed | tf_op | source)
XLA Modules:
  0.0 197.7 jit_solution(11496617834578854245)
XLA Ops:
  6.5 1.8 copy.50
  8.4 0.7 broadcast_compare_fusion
  9.2 0.7 broadcast_select_fusion
  10.0 0.6 dynamic_slice.19
  11.2 0.6 dynamic_slice.18
  12.4 0.8 reshape.278
  13.6 0.7 reshape.277
  14.6 1.2 fusion.62
  15.8 1.3 select_divide_fusion
  17.3 0.9 broadcast_bitcast_fusion.2
  18.2 0.7 fusion.50
  18.9 11.2 %negate_convert_fusion = (bf16[2048,1,256]{2,0,1:T(8,128)(2,1)S(1)}, bf16[2048,1,256]{2,0,1:T(8,128)(2,1)}, bf16[2048,1,256]{2,0,1:T(8,128)(2,1)}) fusion(s32[2048]{0:T(1024)S(1)} %fusion.62, f32[2048]{0:T(1024)S(1)} %select_divide_fusion), kind=kLoop, calls=%fused_computation.16 | loop fusion | flops 10485760 | bytes 3162112 | tf_op jit(solution)/shard_map/convert.7
  30.1 1.2 all-gather.2.cloned.1.call-done
  31.3 1.8 fusion.31
  33.1 0.7 fusion.76
  33.9 1.7 collective-permute-start
  35.6 3.0 %collective-permute-start.1 = (bf16[64,3,2,64]{3,0,2,1:T(8,128)(2,1)}, bf16[64,3,2,64]{3,0,2,1:T(8,128)(2,1)}, u32[]{:S(2)}, u32[]{:S(2)}) collective-permute-start(bf16[64,3,2,64]{3,0,2,1:T(8,128)(2,1)} %get-tuple-element.19), channel_id=1, source_target_pairs={{4,0},{8,4},{12,8},{16,12},{20,16},{24,20},{28,24},{0,28},{5,1},{9... | collective-permute-start | bytes 147464 | tf_op jit(solution)/shard_map/ppermute | solution.py:20
  38.6 1.0 maximum_bitcast_fusion.18
  39.9 1.9 collective-permute-done
  41.8 0.8 collective-permute-done.1
  42.6 1.9 pad_maximum_fusion.1
  44.6 1.6 reshape.279
  47.7 0.8 copy.101
  48.5 3.6 %collective-permute-start.2 = (bf16[64,3,2,512]{3,0,2,1:T(8,128)(2,1)}, bf16[64,3,2,512]{3,0,2,1:T(8,128)(2,1)}, u32[]{:S(2)}, u32[]{:S(2)}) collective-permute-start(bf16[64,3,2,512]{3,0,2,1:T(8,128)(2,1)} %bitcast.193), channel_id=1, source_target_pairs={{4,0},{8,4},{12,8},{16,12},{20,16},{24,20},{28,24},{0,28},{5,1},{9... | collective-permute-start | bytes 1179656 | tf_op jit(solution)/shard_map/ppermute | solution.py:28
  52.5 0.7 broadcast_bitcast_fusion.3
  53.2 0.6 dynamic_slice.20
  55.5 1.6 reshape.276
  57.0 1.2 copy.86
  58.4 0.7 reshape.275
  59.7 2.2 %maximum_bitcast_fusion = (bf16[1,2048,2,256]{3,1,0,2:T(8,128)(2,1)S(1)}, bf16[1,2048,2,256]{3,1,0,2:T(8,128)(2,1)S(1)}) fusion(bf16[2048,1,256]{2,0,1:T(8,128)(2,1)S(1)} %get-tuple-element.26, bf16[2048,1,256]{2,0,1:T(8,128)(2,1)} %get-tuple-element.28, bf16[2048,1,256]{2,0,1:T(8,128)(2,1)} %get-tuple-element.27), kind=kLoop, calls=%fused_computation.14 | loop fusion | flops 2097152 | bytes 7340032 | tf_op jit(solution)/shard_map/stack | solution.py:89
  62.1 8.4 %collective-permute-done.3 = bf16[64,3,2,512]{3,0,2,1:T(8,128)(2,1)} collective-permute-done((bf16[64,3,2,512]{3,0,2,1:T(8,128)(2,1)}, bf16[64,3,2,512]{3,0,2,1:T(8,128)(2,1)}, u32[]{:S(2)}, u32[]{:S(2)}) %collective-permute-start.3) | collective-permute-done | bytes 393248 | tf_op jit(solution)/shard_map/ppermute | solution.py:28
  70.5 6.2 %collective-permute-done.4 = bf16[64,3,2,512]{3,0,2,1:T(8,128)(2,1)} collective-permute-done((bf16[64,3,2,512]{3,0,2,1:T(8,128)(2,1)}, bf16[64,3,2,512]{3,0,2,1:T(8,128)(2,1)}, u32[]{:S(2)}, u32[]{:S(2)}) %collective-permute-start.4) | collective-permute-done | bytes 393248 | tf_op jit(solution)/shard_map/ppermute | solution.py:28
  76.7 2.3 %fusion.36 = f32[64,3,2,256]{3,0,2,1:T(8,128)S(1)} fusion(bf16[64,3,2,512]{3,0,2,1:T(8,128)(2,1)} %collective-permute-done.4, bf16[64,3,2,512]{3,0,2,1:T(8,128)(2,1)} %collective-permute-done.3, bf16[64,3,2,512]{3,0,2,1:T(8,128)(2,1)} %collective-permute-done.2, bf16[64,3,2,512]{3,0,2,1:T(8,128)(2,1)} %bitcast.193, ...), kind=kOutput, calls=%fused_computation.44 | convolution fusion | flops 819986432 | bytes 6160384 | tf_op jit(solution)/shard_map/hwcp,cpdk->hwdk/dot_general | solution.py:93
  79.0 1.0 fusion.60
  80.0 1.7 bitcast_convert_fusion.1
  81.9 10.1 %collective-permute-start.5 = (bf16[64,3,2,512]{3,0,2,1:T(8,128)(2,1)S(1)}, bf16[64,3,2,512]{3,0,2,1:T(8,128)(2,1)S(1)}, u32[]{:S(2)}, u32[]{:S(2)}) collective-permute-start(bf16[64,3,2,512]{3,0,2,1:T(8,128)(2,1)S(1)} %get-tuple-element.5), channel_id=1, source_target_pairs={{28,0},{0,4},{4,8},{8,12},{12,16},{16,20},{20,24},{24,28},{29,1},{... | collective-permute-start | bytes 1179656 | tf_op jit(solution)/shard_map/ppermute | solution.py:28
  92.1 13.4 %collective-permute-done.5 = bf16[64,3,2,512]{3,0,2,1:T(8,128)(2,1)S(1)} collective-permute-done((bf16[64,3,2,512]{3,0,2,1:T(8,128)(2,1)S(1)}, bf16[64,3,2,512]{3,0,2,1:T(8,128)(2,1)S(1)}, u32[]{:S(2)}, u32[]{:S(2)}) %collective-permute-start.5) | collective-permute-done | bytes 393248 | tf_op jit(solution)/shard_map/ppermute | solution.py:28
  105.5 0.5 collective-permute-done.6
  106.0 24.1 %collective-permute-done.7 = bf16[64,3,2,512]{3,0,2,1:T(8,128)(2,1)S(1)} collective-permute-done((bf16[64,3,2,512]{3,0,2,1:T(8,128)(2,1)S(1)}, bf16[64,3,2,512]{3,0,2,1:T(8,128)(2,1)S(1)}, u32[]{:S(2)}, u32[]{:S(2)}) %collective-permute-start.7) | collective-permute-done | bytes 393248 | tf_op jit(solution)/shard_map/ppermute | solution.py:28
  130.5 4.7 %collective-permute-start.9 = (bf16[64,3,2,64]{3,0,2,1:T(8,128)(2,1)S(1)}, bf16[64,3,2,64]{3,0,2,1:T(8,128)(2,1)S(1)}, u32[]{:S(2)}, u32[]{:S(2)}) collective-permute-start(bf16[64,3,2,64]{3,0,2,1:T(8,128)(2,1)S(1)} %get-tuple-element.17), channel_id=1, source_target_pairs={{4,0},{8,4},{12,8},{16,12},{20,16},{24,20},{28,24},{0,28},{5,1},{9... | collective-permute-start | bytes 147464 | tf_op jit(solution)/shard_map/ppermute | solution.py:20
  135.2 0.8 maximum_bitcast_fusion.16
  136.0 1.9 collective-permute-done.8
  138.2 0.6 reshape.280
  140.6 0.6 fusion.22
  141.3 3.1 %copy.60 = bf16[256,3,2,512]{3,2,1,0:T(2,128)(2,1)} copy(bf16[256,3,2,512]{0,3,2,1:T(8,128)(2,1)S(1)} %fusion.22) | data formatting | bytes 3145728 | tf_op jit(solution)/shard_map/convert_element_type | solution.py:161
  144.4 0.6 dynamic-slice
  145.7 43.0 %all-reduce.7.cloned.1.call-done = bf16[256,3,2,512]{3,2,1,0:T(2,128)(2,1)} async-done(((bf16[256,3,2,512]{3,2,1,0:T(2,128)(2,1)}), bf16[256,3,2,512]{3,2,1,0:T(2,128)(2,1)}) %all-reduce.7.cloned.1.call-update) | async-done | bytes 1572880
  188.7 2.1 %dynamic-slice_convert_fusion = f32[64,3,2,512]{3,2,1,0:T(2,128)} fusion(bf16[256,3,2,512]{3,2,1,0:T(2,128)(2,1)} %all-reduce.7.cloned.1.call-done, u32[]{:T(128)S(6)} %multiply.1), kind=kLoop, calls=%fused_computation.71 | loop fusion | flops 196608 | bytes 1179652 | tf_op jit(solution)/shard_map/convert_element_type | solution.py:165
  (77 shorter events, 7.3 us)
Async XLA Ops:
  6.5 3.5 %copy-start.7 = (s32[8]{0:T(128)S(1)}, s32[8]{0:T(128)}, u32[]{:S(2)}) copy-start(s32[8]{0:T(128)} %param.13) | copy-start | bytes 100
  6.5 4.7 %copy-start.8 = (s32[8]{0:T(128)S(1)}, s32[8]{0:T(128)}, u32[]{:S(2)}) copy-start(s32[8]{0:T(128)} %param.12) | copy-start | bytes 100
  6.5 24.8 %all-gather.2.cloned.1.call-start = ((), (), s32[]{:S(2)}) async-start(), calls=%async_computation | async-start | bytes 1966080 | tf_op jit(solution)/shard_map/all_gather | solution.py:123
  8.4 180.3 %all-reduce.7.cloned.1.call-start = ((), (), s32[]{:S(2)}) async-start(), calls=%async_computation.1 | async-start | bytes 3145728
  12.4 4.7 %copy-start.2 = (bf16[3,2,256,256]{3,2,1,0:T(8,128)(2,1)S(1)}, bf16[3,2,256,256]{3,2,1,0:T(8,128)(2,1)}, u32[]{:S(2)}) copy-start(bf16[3,2,256,256]{3,2,1,0:T(8,128)(2,1)} %param.9) | copy-start | bytes 2359300
  31.3 7.3 %copy-start.3 = (bf16[3,1,128,256]{3,2,1,0:T(8,128)(2,1)S(1)}, bf16[3,1,128,256]{3,2,1,0:T(8,128)(2,1)}, u32[]{:S(2)}) copy-start(bf16[3,1,128,256]{3,2,1,0:T(8,128)(2,1)} %get-tuple-element.30) | copy-start | bytes 589828
  33.9 7.9 %collective-permute-start = (bf16[64,3,2,64]{3,0,2,1:T(8,128)(2,1)}, bf16[64,3,2,64]{3,0,2,1:T(8,128)(2,1)S(1)}, u32[]{:S(2)}, u32[]{:S(2)}) collective-permute-start(bf16[64,3,2,64]{3,0,2,1:T(8,128)(2,1)} %get-tuple-element.18), channel_id=1, source_target_pairs={{0,4},{4,8},{8,12},{12,16},{16,20},{20,24},{24,28},{28,0},{1,5},{5... | collective-permute-start | bytes 147464 | tf_op jit(solution)/shard_map/ppermute | solution.py:19
  35.6 7.0 %collective-permute-start.1 = (bf16[64,3,2,64]{3,0,2,1:T(8,128)(2,1)}, bf16[64,3,2,64]{3,0,2,1:T(8,128)(2,1)}, u32[]{:S(2)}, u32[]{:S(2)}) collective-permute-start(bf16[64,3,2,64]{3,0,2,1:T(8,128)(2,1)} %get-tuple-element.19), channel_id=1, source_target_pairs={{4,0},{8,4},{12,8},{16,12},{20,16},{24,20},{28,24},{0,28},{5,1},{9... | collective-permute-start | bytes 147464 | tf_op jit(solution)/shard_map/ppermute | solution.py:20
  46.2 1.0 copy-start.4
  46.2 1.1 copy-start.5
  47.3 5.9 %copy-start.9 = (s32[8]{0:T(128)S(1)}, s32[8]{0:T(128)}, u32[]{:S(2)}) copy-start(s32[8]{0:T(128)} %param.14) | copy-start | bytes 100
  47.3 7.6 %copy-start.1 = (f32[1,3,128,384]{3,2,1,0:T(8,128)S(1)}, f32[1,3,128,384]{3,2,1,0:T(8,128)}, u32[]{:S(2)}) copy-start(f32[1,3,128,384]{3,2,1,0:T(8,128)} %broadcast_bitcast_fusion.2) | copy-start | bytes 1769476
  48.5 13.6 %collective-permute-start.2 = (bf16[64,3,2,512]{3,0,2,1:T(8,128)(2,1)}, bf16[64,3,2,512]{3,0,2,1:T(8,128)(2,1)}, u32[]{:S(2)}, u32[]{:S(2)}) collective-permute-start(bf16[64,3,2,512]{3,0,2,1:T(8,128)(2,1)} %bitcast.193), channel_id=1, source_target_pairs={{4,0},{8,4},{12,8},{16,12},{20,16},{24,20},{28,24},{0,28},{5,1},{9... | collective-permute-start | bytes 1179656 | tf_op jit(solution)/shard_map/ppermute | solution.py:28
  52.2 18.4 %collective-permute-start.3 = (bf16[64,3,2,512]{3,0,2,1:T(8,128)(2,1)}, bf16[64,3,2,512]{3,0,2,1:T(8,128)(2,1)}, u32[]{:S(2)}, u32[]{:S(2)}) collective-permute-start(bf16[64,3,2,512]{3,0,2,1:T(8,128)(2,1)} %bitcast.193), channel_id=1, source_target_pairs={{8,0},{12,4},{16,8},{20,12},{24,16},{28,20},{0,24},{4,28},{9,1},{1... | collective-permute-start | bytes 1179656 | tf_op jit(solution)/shard_map/ppermute | solution.py:28
  52.4 24.3 %collective-permute-start.4 = (bf16[64,3,2,512]{3,0,2,1:T(8,128)(2,1)}, bf16[64,3,2,512]{3,0,2,1:T(8,128)(2,1)}, u32[]{:S(2)}, u32[]{:S(2)}) collective-permute-start(bf16[64,3,2,512]{3,0,2,1:T(8,128)(2,1)} %bitcast.193), channel_id=1, source_target_pairs={{12,0},{16,4},{20,8},{24,12},{28,16},{0,20},{4,24},{8,28},{13,1},{... | collective-permute-start | bytes 1179656 | tf_op jit(solution)/shard_map/ppermute | solution.py:28
  81.8 10.3 %copy-start = (f32[3,128,383]{2,1,0:T(8,128)S(1)}, f32[3,128,383]{2,1,0:T(8,128)}, u32[]{:S(2)}) copy-start(f32[3,128,383]{2,1,0:T(8,128)} %reshape.276) | copy-start | bytes 1764868
  81.9 23.6 %collective-permute-start.5 = (bf16[64,3,2,512]{3,0,2,1:T(8,128)(2,1)S(1)}, bf16[64,3,2,512]{3,0,2,1:T(8,128)(2,1)S(1)}, u32[]{:S(2)}, u32[]{:S(2)}) collective-permute-start(bf16[64,3,2,512]{3,0,2,1:T(8,128)(2,1)S(1)} %get-tuple-element.5), channel_id=1, source_target_pairs={{28,0},{0,4},{4,8},{8,12},{12,16},{16,20},{20,24},{24,28},{29,1},{... | collective-permute-start | bytes 1179656 | tf_op jit(solution)/shard_map/ppermute | solution.py:28
  92.0 14.0 %collective-permute-start.6 = (bf16[64,3,2,512]{3,0,2,1:T(8,128)(2,1)S(1)}, bf16[64,3,2,512]{3,0,2,1:T(8,128)(2,1)S(1)}, u32[]{:S(2)}, u32[]{:S(2)}) collective-permute-start(bf16[64,3,2,512]{3,0,2,1:T(8,128)(2,1)S(1)} %get-tuple-element.7), channel_id=1, source_target_pairs={{24,0},{28,4},{0,8},{4,12},{8,16},{12,20},{16,24},{20,28},{25,1},{... | collective-permute-start | bytes 1179656 | tf_op jit(solution)/shard_map/ppermute | solution.py:28
  92.0 38.1 %collective-permute-start.7 = (bf16[64,3,2,512]{3,0,2,1:T(8,128)(2,1)S(1)}, bf16[64,3,2,512]{3,0,2,1:T(8,128)(2,1)S(1)}, u32[]{:S(2)}, u32[]{:S(2)}) collective-permute-start(bf16[64,3,2,512]{3,0,2,1:T(8,128)(2,1)S(1)} %get-tuple-element.6), channel_id=1, source_target_pairs={{20,0},{24,4},{28,8},{0,12},{4,16},{8,20},{12,24},{16,28},{21,1},{... | collective-permute-start | bytes 1179656 | tf_op jit(solution)/shard_map/ppermute | solution.py:28
  130.4 7.5 %collective-permute-start.8 = (bf16[64,3,2,64]{3,0,2,1:T(8,128)(2,1)S(1)}, bf16[64,3,2,64]{3,0,2,1:T(8,128)(2,1)S(1)}, u32[]{:S(2)}, u32[]{:S(2)}) collective-permute-start(bf16[64,3,2,64]{3,0,2,1:T(8,128)(2,1)S(1)} %get-tuple-element.16), channel_id=1, source_target_pairs={{0,4},{4,8},{8,12},{12,16},{16,20},{20,24},{24,28},{28,0},{1,5},{5... | collective-permute-start | bytes 147464 | tf_op jit(solution)/shard_map/ppermute | solution.py:19
  130.5 7.4 %collective-permute-start.9 = (bf16[64,3,2,64]{3,0,2,1:T(8,128)(2,1)S(1)}, bf16[64,3,2,64]{3,0,2,1:T(8,128)(2,1)S(1)}, u32[]{:S(2)}, u32[]{:S(2)}) collective-permute-start(bf16[64,3,2,64]{3,0,2,1:T(8,128)(2,1)S(1)} %get-tuple-element.17), channel_id=1, source_target_pairs={{4,0},{8,4},{12,8},{16,12},{20,16},{24,20},{28,24},{0,28},{5,1},{9... | collective-permute-start | bytes 147464 | tf_op jit(solution)/shard_map/ppermute | solution.py:20
  138.8 1.0 copy-start.6
  141.3 3.2 %copy-start.10 = (u32[32]{0:T(128)S(1)}, u32[32]{0:T(128)}, u32[]{:S(2)}) copy-start(u32[32]{0:T(128)} %constant.78) | copy-start | bytes 388
Sparse Core Ops, SparseCore 0:
  8.9 22.3 all-gather.1
  144.5 44.0 all-reduce.6
where the time goes:
time: 198 us
  waiting for transfers between devices  102 us (52%)
  other arithmetic  24.9 us (13%)
  starting transfers between devices  23.6 us (12%)
  local copies, waits for them, and re-layouts  23.3 us (12%)
  between operations  16.8 us (8%)
  matrix products  7.33 us (4%)
    ppermute x6, waiting for transfers between devices, from_behind(): return lax.ppermute(block, axis, route)  52.7 us
    unnamed x3, waiting for transfers between devices  43 us
    ppermute x6, starting transfers between devices, from_behind(): return lax.ppermute(block, axis, route)  14 us
    another operation x1, other arithmetic  11.2 us
    unnamed x43, local copies, waits for them, and re-layouts  8.28 us
    ppermute x2, starting transfers between devices, with_halo(): after = lax.ppermute(initial, axis, down)  7.75 us
  transfers between devices with their start and end apart: 12, of which 11 were waited for; matrix products, arithmetic and copies ran while one was open for 16% of the time, Pallas kernels for 0%

commit v1 on v0

--- a/solution.py
+++ b/solution.py
@@ -2,6 +2,8 @@
 
 import jax
 import jax.numpy as jnp
+import ml_dtypes
+import numpy as np
 from jax import lax
 from jax.sharding import PartitionSpec as P
 
@@ -71,33 +73,21 @@
     return result.reshape(row_count, wave_count, part_count, block_count * block_size)
 
 
-def spectrum_table(offset, span_width, az_count):
-    places = jnp.arange(4 * az_count, dtype=jnp.int32) - offset
+def taper_row(offset, span_width, length):
+    places = jnp.arange(length, dtype=jnp.int32) - offset
     inside = (places >= 0) & (places < span_width)
     places = jnp.where(inside, places, 0)
-    frequency = jnp.arange(FREQS, dtype=jnp.int32)
-    phases = jnp.mod(places[:, None] * frequency[None, :], FREQS).astype(jnp.float32) * (
-        2.0 * math.pi / FREQS
-    )
     span_float = span_width.astype(jnp.float32)
     taper = 0.5 - 0.5 * jnp.cos((places.astype(jnp.float32) + 0.5) * (2.0 * math.pi) / span_float)
-    taper = jnp.where(inside, taper, 0.0) / jnp.sqrt(span_float)
-    cosine = taper[:, None] * jnp.cos(phases)
-    sine = taper[:, None] * jnp.sin(phases)
-    upper = jnp.stack([cosine, -sine], axis=1)
-    lower = jnp.stack([sine, cosine], axis=1)
-    return jnp.stack([upper, lower], axis=0).astype(jnp.bfloat16)
+    return jnp.where(inside, taper, 0.0) / jnp.sqrt(span_float)
 
 
-def view_slopes(window, spectra_table, target_plane):
-    spectrum = jnp.einsum(
-        "hwcp,cpdk->hwdk", window, spectra_table, preferred_element_type=jnp.float32
-    )
-    power = spectrum[:, :, 0] * spectrum[:, :, 0] + spectrum[:, :, 1] * spectrum[:, :, 1]
-    misfit = power - target_plane
-    slope = (2.0 * misfit[:, :, None, :] * spectrum).astype(jnp.bfloat16)
-    back = jnp.einsum("hwdk,cpdk->hwcp", slope, spectra_table, preferred_element_type=jnp.float32)
-    return back.astype(jnp.bfloat16)
+def dft_pair():
+    index = np.arange(FREQS)
+    phases = (index[:, None] * index[None, :] % FREQS) * (2.0 * np.pi / FREQS)
+    cosine, sine = np.cos(phases), np.sin(phases)
+    table = np.stack([np.stack([cosine, -sine], axis=1), np.stack([sine, cosine], axis=1)], axis=0)
+    return table.astype(ml_dtypes.bfloat16)
 
 
 def on_device(
@@ -128,29 +118,37 @@
     backward = toeplitz(masked_taps[:, 0, ::-1], -masked_taps[:, 1, ::-1])
     extended = with_halo(height_field, (("az", 3),), REACH)
     hologram = convolve(extended, forward).astype(jnp.bfloat16)
-    home_lead = 0
-    sector = jnp.mod(lax.axis_index("az") - home_lead, loop_size)
-    relatives = [position - home_lead for position in range(4)]
-    blocks = []
-    for relative in relatives:
-        if relative == 0:
-            blocks.append(hologram)
-        else:
-            blocks.append(from_behind(hologram, "az", -relative))
-    window = jnp.concatenate(blocks, axis=3)
-    offset = lax.dynamic_index_in_dim(sector_offset, sector, 0, False)
-    span_width = lax.dynamic_index_in_dim(sector_width, sector, 0, False)
-    pattern = lax.dynamic_index_in_dim(target_index, sector, 0, False)
+    here = lax.axis_index("az")
+    rows, waves, parts, length = hologram.shape
+    tapers = []
+    for back in range(4):
+        sector = jnp.mod(here - back, loop_size)
+        row = taper_row(sector_offset[sector], sector_width[sector], 4 * length)
+        tapers.append(row[back * length : (back + 1) * length])
+    wide = hologram.astype(jnp.float32)
+    folded = jnp.zeros((rows, waves, parts, FREQS), jnp.float32)
+    for back in range(4):
+        part = (wide * tapers[back]).reshape(rows, waves, parts, length // FREQS, FREQS)
+        part = jnp.sum(part, axis=3)
+        if back:
+            part = from_behind(part.astype(jnp.bfloat16), "az", -back).astype(jnp.float32)
+        folded = folded + part
+    table = jnp.asarray(dft_pair())
+    pattern = target_index[here]
     target_plane = lax.dynamic_index_in_dim(target_maps, pattern, 0, False)
-    spectra_table = spectrum_table(offset, span_width, az_count)
-    slopes = view_slopes(window, spectra_table, target_plane)
+    spectrum = jnp.einsum(
+        "hwcp,cpdk->hwdk", folded.astype(jnp.bfloat16), table, preferred_element_type=jnp.float32
+    )
+    power = spectrum[:, :, 0] * spectrum[:, :, 0] + spectrum[:, :, 1] * spectrum[:, :, 1]
+    misfit = power - target_plane
+    slope = (2.0 * misfit[:, :, None, :] * spectrum).astype(jnp.bfloat16)
+    returned = jnp.einsum("hwdk,cpdk->hwcp", slope, table, preferred_element_type=jnp.float32)
+    returned = returned.astype(jnp.bfloat16)
     summed = zero_field
-    for position, relative in enumerate(relatives):
-        portion = slopes[..., position * az_count : (position + 1) * az_count]
-        if relative == 0:
-            summed = portion.astype(jnp.float32)
-        else:
-            summed = summed + from_behind(portion, "az", relative).astype(jnp.float32)
+    for back in range(4):
+        part = from_behind(returned, "az", back) if back else returned
+        part = jnp.tile(part.astype(jnp.float32), (1, 1, 1, length // FREQS))
+        summed = summed + part * tapers[back]
     hologram_grad = summed.astype(jnp.bfloat16)
     grad_extended = with_halo(hologram_grad, (("az", 3),), REACH)
     field_grad = convolve(grad_extended, backward).astype(jnp.bfloat16)

time: 198 us -> 183 us (0.924)
  waiting for transfers between devices: 102 us -> 65.1 us
  other arithmetic: 24.9 us -> 38.8 us
  local copies, waits for them, and re-layouts: 23.3 us -> 34.6 us
  starting transfers between devices: 23.6 us -> 20 us
  matrix products: 7.33 us -> 3.81 us
  between operations: 16.8 us -> 19.3 us
    ppermute x6, waiting for transfers between devices: 52.7 us -> 20.9 us  [from_behind(): return lax.ppermute(block, axis, route)]
    another operation x0 -> x8, local copies, waits for them, and re-layouts: none -> 14 us  [on_device(): part = jnp.tile(part.astype(jnp.float32), (1, 1, 1, length // FREQS))]
    another operation x2 -> x0, other arithmetic: 13.4 us -> none
    and x0 -> x8, other arithmetic: none -> 11 us  [taper_row(): inside = (places >= 0) & (places < span_width)]
    mul x1 -> x9, other arithmetic: 0.97 us -> 10.9 us  [the longest x8 9.91 us: taper_row(): (places.astype(jnp.float32) + 0.5) * (2.0 * math.pi) / span_float]
    ppermute x6, starting transfers between devices: 14 us -> 8.92 us  [from_behind(): return lax.ppermute(block, axis, route)]
    reduce_sum x0 -> x1, other arithmetic: none -> 4.67 us  [on_device(): part = jnp.sum(part, axis=3)]
    dot_general x2, matrix products: 4.07 us -> 0.6 us  [the longest x1 0.33 us: on_device(): jnp.einsum('hwdk,cpdk->hwcp', slope, table, preferred_element_type=jnp.fl...]
  transfers between devices with their start and end apart: 12 -> 12, of which waited for: 11 -> 7; matrix products, arithmetic and copies ran while one was open for 16% -> 26% of each run, Pallas kernels for 0% -> 0%
where the time goes in v1:
time: 183 us; the launch traced here: 182 us
  waiting for transfers between devices  65.1 us (36%)
  other arithmetic  38.8 us (21%)
  local copies, waits for them, and re-layouts  34.6 us (19%)
  starting transfers between devices  20 us (11%)
  between operations  19.3 us (11%)
  matrix products  3.81 us (2%)
    unnamed x3, waiting for transfers between devices  42.5 us
    ppermute x6, waiting for transfers between devices, from_behind(): return lax.ppermute(block, axis, route)  20.9 us
    another operation x8, local copies, waits for them, and re-layouts, on_device(): part = jnp.tile(part.astype(jnp.float32), (1, 1, 1, length // FREQS))  14 us
    and x8, other arithmetic, taper_row(): inside = (places >= 0) & (places < span_width)  11 us
    mul x8, other arithmetic, taper_row(): (places.astype(jnp.float32) + 0.5) * (2.0 * math.pi) / span_float  9.91 us
    ppermute x6, starting transfers between devices, from_behind(): return lax.ppermute(block, axis, route)  8.92 us
    ppermute x2, starting transfers between devices, with_halo(): after = lax.ppermute(initial, axis, down)  8 us
    unnamed x53, local copies, waits for them, and re-layouts  6.66 us
  transfers between devices with their start and end apart: 12, of which 7 were waited for; matrix products, arithmetic and copies ran while one was open for 26% of the time, Pallas kernels for 0%

profile of v1, /device:TPU:0, one launch (start us, length us, event | category | flops | bytes accessed | tf_op | source)
XLA Modules:
  0.0 181.7 jit_solution(9889622206623541078)
XLA Ops:
  6.5 1.9 %copy.69 = bf16[64,3,2,512]{3,0,2,1:T(8,128)(2,1)} copy(bf16[64,3,2,512]{3,2,1,0:T(2,128)(2,1)} %param.9) | data formatting | bytes 786432 | tf_op args[0]
  8.6 1.5 fusion.119
  10.1 1.3 add_multiply_fusion.7
  11.4 1.3 fusion.69
  12.7 1.2 add_multiply_fusion.6
  13.9 1.2 fusion.68
  15.1 1.2 add_multiply_fusion.5
  16.3 1.2 fusion.67
  17.5 1.3 add_multiply_fusion.4
  18.8 1.3 fusion.66
  21.5 1.3 add_multiply_fusion.3
  22.8 1.3 fusion.70
  24.1 1.2 add_multiply_fusion.2
  25.3 1.2 fusion.71
  26.5 1.2 add_multiply_fusion.1
  31.1 0.9 maximum_bitcast_fusion.12
  32.1 1.7 fusion.72
  38.1 1.5 reshape.125
  39.6 1.3 add_multiply_fusion
  42.6 0.8 fusion.31
  43.4 1.8 fusion.13
  45.3 3.0 %collective-permute-start = (bf16[64,3,2,64]{3,0,2,1:T(8,128)(2,1)S(1)}, bf16[64,3,2,64]{3,0,2,1:T(8,128)(2,1)S(1)}, u32[]{:S(2)}, u32[]{:S(2)}) collective-permute-start(bf16[64,3,2,64]{3,0,2,1:T(8,128)(2,1)S(1)} %get-tuple-element.17), channel_id=1, source_target_pairs={{0,4},{4,8},{8,12},{12,16},{16,20},{20,24},{24,28},{28,0},{1,5},{5... | collective-permute-start | bytes 147464 | tf_op jit(solution)/shard_map/ppermute | solution.py:21
  48.3 3.3 %collective-permute-start.1 = (bf16[64,3,2,64]{3,0,2,1:T(8,128)(2,1)S(1)}, bf16[64,3,2,64]{3,0,2,1:T(8,128)(2,1)S(1)}, u32[]{:S(2)}, u32[]{:S(2)}) collective-permute-start(bf16[64,3,2,64]{3,0,2,1:T(8,128)(2,1)S(1)} %get-tuple-element.18), channel_id=1, source_target_pairs={{4,0},{8,4},{12,8},{16,12},{20,16},{24,20},{28,24},{0,28},{5,1},{9... | collective-permute-start | bytes 147464 | tf_op jit(solution)/shard_map/ppermute | solution.py:22
  51.6 1.9 %fusion.73 = pred[2048]{0:T(1024)(128)(4,1)} fusion(s32[]{:T(128)} %bitcast.40, s32[]{:T(128)} %bitcast.39), kind=kLoop, calls=%fused_computation.122 | loop fusion | flops 8192 | bytes 2056 | tf_op jit(solution)/shard_map/and | solution.py:78
  59.5 4.7 %multiply_reduce_fusion.3 = (f32[64,3,2,256]{3,2,1,0:T(2,128)S(1)}, bf16[64,3,2,256]{3,2,1,0:T(2,128)(2,1)S(1)}, bf16[64,3,2,256]{3,2,1,0:T(2,128)(2,1)S(1)}, bf16[64,3,2,256]{3,2,1,0:T(2,128)(2,1)S(1)}) fusion(f32[64,3,2,2,256]{4,3,2,1,0:T(2,128)S(1)} %reshape.133, f32[2,256]{1,0:T(2,128)S(1)} %fusion.74, f32[2,256]{1,0:T(2,128)S(1)} %fusion.77, ...), kind=kLoop, calls=%fused_computation.37 | loop fusion | flops 1179648 | bytes 1777664 | tf_op jit(solution)/shard_map/reduce_sum | solution.py:132
  64.2 3.0 %collective-permute-start.2 = (bf16[64,3,2,256]{3,0,2,1:T(8,128)(2,1)S(1)}, bf16[64,3,2,256]{3,0,2,1:T(8,128)(2,1)S(1)}, u32[]{:S(2)}, u32[]{:S(2)}) collective-permute-start(bf16[64,3,2,256]{3,0,2,1:T(8,128)(2,1)S(1)} %copy.130), channel_id=1, source_target_pairs={{4,0},{8,4},{12,8},{16,12},{20,16},{24,20},{28,24},{0,28},{5,1},{9... | collective-permute-start | bytes 589832 | tf_op jit(solution)/shard_map/ppermute | solution.py:30
  67.5 1.3 fusion.108
  68.8 3.9 %collective-permute-done.2 = bf16[64,3,2,256]{3,0,2,1:T(8,128)(2,1)S(1)} collective-permute-done((bf16[64,3,2,256]{3,0,2,1:T(8,128)(2,1)S(1)}, bf16[64,3,2,256]{3,0,2,1:T(8,128)(2,1)S(1)}, u32[]{:S(2)}, u32[]{:S(2)}) %collective-permute-start.2) | collective-permute-done | bytes 196640 | tf_op jit(solution)/shard_map/ppermute | solution.py:30
  72.7 4.0 %collective-permute-done.3 = bf16[64,3,2,256]{3,0,2,1:T(8,128)(2,1)S(1)} collective-permute-done((bf16[64,3,2,256]{3,0,2,1:T(8,128)(2,1)S(1)}, bf16[64,3,2,256]{3,0,2,1:T(8,128)(2,1)S(1)}, u32[]{:S(2)}, u32[]{:S(2)}) %collective-permute-start.3) | collective-permute-done | bytes 196640 | tf_op jit(solution)/shard_map/ppermute | solution.py:30
  76.7 2.1 %collective-permute-done.4 = bf16[64,3,2,256]{3,0,2,1:T(8,128)(2,1)S(1)} collective-permute-done((bf16[64,3,2,256]{3,0,2,1:T(8,128)(2,1)S(1)}, bf16[64,3,2,256]{3,0,2,1:T(8,128)(2,1)S(1)}, u32[]{:S(2)}, u32[]{:S(2)}) %collective-permute-start.4) | collective-permute-done | bytes 196640 | tf_op jit(solution)/shard_map/ppermute | solution.py:30
  79.0 1.0 fusion.44
  80.4 5.8 %collective-permute-start.5 = (bf16[64,3,2,256]{3,0,2,1:T(8,128)(2,1)S(1)}, bf16[64,3,2,256]{3,0,2,1:T(8,128)(2,1)}, u32[]{:S(2)}, u32[]{:S(2)}) collective-permute-start(bf16[64,3,2,256]{3,0,2,1:T(8,128)(2,1)S(1)} %fusion.17), channel_id=1, source_target_pairs={{28,0},{0,4},{4,8},{8,12},{12,16},{16,20},{20,24},{24,28},{29,1},{... | collective-permute-start | bytes 589832 | tf_op jit(solution)/shard_map/ppermute | solution.py:30
  86.1 1.3 fusion.109
  88.3 7.4 %collective-permute-done.5 = bf16[64,3,2,256]{3,0,2,1:T(8,128)(2,1)} collective-permute-done((bf16[64,3,2,256]{3,0,2,1:T(8,128)(2,1)S(1)}, bf16[64,3,2,256]{3,0,2,1:T(8,128)(2,1)}, u32[]{:S(2)}, u32[]{:S(2)}) %collective-permute-start.5) | collective-permute-done | bytes 196640 | tf_op jit(solution)/shard_map/ppermute | solution.py:30
  95.7 2.0 %tile.82 = f32[64,3,2,2,256]{4,3,0,2,1:T(2,128)} broadcast(bf16[64,3,2,256]{3,0,2,1:T(8,128)(2,1)} %collective-permute-done.5), dimensions={0,1,2,4} | broadcast | bytes 983040 | tf_op jit(solution)/shard_map/tile | solution.py:150
  97.7 1.8 tile.83
  99.5 2.0 %tile.84 = f32[64,3,2,2,256]{4,3,0,2,1:T(2,128)} broadcast(bf16[64,3,2,256]{3,0,2,1:T(8,128)(2,1)} %collective-permute-done.6), dimensions={0,1,2,4} | broadcast | bytes 983040 | tf_op jit(solution)/shard_map/tile | solution.py:150
  101.5 2.7 %tile.85 = f32[64,3,2,512]{3,0,2,1:T(8,128)} reshape(f32[64,3,2,2,256]{4,3,0,2,1:T(2,128)} %tile.84) | data formatting | bytes 1572864 | tf_op jit(solution)/shard_map/tile | solution.py:150
  104.1 3.5 %collective-permute-done.7 = bf16[64,3,2,256]{3,0,2,1:T(8,128)(2,1)} collective-permute-done((bf16[64,3,2,256]{3,0,2,1:T(8,128)(2,1)S(1)}, bf16[64,3,2,256]{3,0,2,1:T(8,128)(2,1)}, u32[]{:S(2)}, u32[]{:S(2)}) %collective-permute-start.7) | collective-permute-done | bytes 196640 | tf_op jit(solution)/shard_map/ppermute | solution.py:30
  107.6 2.0 %tile.86 = f32[64,3,2,2,256]{4,3,0,2,1:T(2,128)} broadcast(bf16[64,3,2,256]{3,0,2,1:T(8,128)(2,1)} %collective-permute-done.7), dimensions={0,1,2,4} | broadcast | bytes 983040 | tf_op jit(solution)/shard_map/tile | solution.py:150
  109.6 2.7 %tile.87 = f32[64,3,2,512]{3,0,2,1:T(8,128)} reshape(f32[64,3,2,2,256]{4,3,0,2,1:T(2,128)} %tile.86) | data formatting | bytes 1572864 | tf_op jit(solution)/shard_map/tile | solution.py:150
  112.4 1.8 %add_convert_fusion = bf16[64,3,2,512]{3,0,2,1:T(8,128)(2,1)S(1)} fusion(f32[64,3,2,512]{3,0,2,1:T(8,128)} %tile.87, f32[64,3,2,512]{3,0,2,1:T(8,128)} %tile.85, f32[64,3,2,512]{3,0,2,1:T(8,128)S(1)} %tile.83, f32[64,3,2,512]{3,0,2,1:T(8,128)S(1)} %tile.81, f32[512]{0:T(512)S(1)} %copy-done.13, f32[512]{0:T(512)S(1)} %copy-done.12, f32[512]{0:T(512)S(1)} %copy-done.11, ...), kind=kLoop, calls=%fused_computation.33 | loop fusion | flops 1572864 | bytes 3547136 | tf_op jit(solution)/shard_map/convert_element_type | solution.py:152
  114.3 4.7 %collective-permute-start.9 = (bf16[64,3,2,64]{3,0,2,1:T(8,128)(2,1)S(1)}, bf16[64,3,2,64]{3,0,2,1:T(8,128)(2,1)S(1)}, u32[]{:S(2)}, u32[]{:S(2)}) collective-permute-start(bf16[64,3,2,64]{3,0,2,1:T(8,128)(2,1)S(1)} %get-tuple-element.16), channel_id=1, source_target_pairs={{4,0},{8,4},{12,8},{16,12},{20,16},{24,20},{28,24},{0,28},{5,1},{9... | collective-permute-start | bytes 147464 | tf_op jit(solution)/shard_map/ppermute | solution.py:22
  119.1 0.9 maximum_bitcast_fusion.10
  120.0 1.8 collective-permute-done.8
  125.2 3.1 %copy.82 = bf16[256,3,2,512]{3,2,1,0:T(2,128)(2,1)} copy(bf16[256,3,2,512]{0,3,2,1:T(8,128)(2,1)S(1)} %fusion.2) | data formatting | bytes 3145728 | tf_op jit(solution)/shard_map/convert_element_type | solution.py:159
  130.2 42.5 %all-reduce.7.cloned.1.call-done = bf16[256,3,2,512]{3,2,1,0:T(2,128)(2,1)} async-done(((bf16[256,3,2,512]{3,2,1,0:T(2,128)(2,1)}), bf16[256,3,2,512]{3,2,1,0:T(2,128)(2,1)}) %all-reduce.7.cloned.1.call-update) | async-done | bytes 1572880
  172.7 2.1 %dynamic-slice_convert_fusion = f32[64,3,2,512]{3,2,1,0:T(2,128)} fusion(bf16[256,3,2,512]{3,2,1,0:T(2,128)(2,1)} %all-reduce.7.cloned.1.call-done, u32[]{:T(128)S(6)} %multiply.5), kind=kLoop, calls=%fused_computation.48 | loop fusion | flops 196608 | bytes 1179652 | tf_op jit(solution)/shard_map/convert_element_type | solution.py:163
  (118 shorter events, 18.8 us)
Async XLA Ops:
  6.5 21.2 %copy-start = (bf16[3,2,256,256]{3,2,1,0:T(8,128)(2,1)S(1)}, bf16[3,2,256,256]{3,2,1,0:T(8,128)(2,1)}, u32[]{:S(2)}) copy-start(bf16[3,2,256,256]{3,2,1,0:T(8,128)(2,1)} %param.10) | copy-start | bytes 2359300
  6.5 36.9 %all-gather.2.cloned.1.call-start = ((), (), s32[]{:S(2)}) async-start(), calls=%async_computation | async-start | bytes 1966080 | tf_op jit(solution)/shard_map/all_gather | solution.py:113
  8.5 164.2 %all-reduce.7.cloned.1.call-start = ((), (), s32[]{:S(2)}) async-start(), calls=%async_computation.1 | async-start | bytes 3145728
  40.9 1.7 copy-start.1
  43.4 10.0 %copy-start.14 = (s32[8]{0:T(128)S(1)}, s32[8]{0:T(128)}, u32[]{:S(2)}) copy-start(s32[8]{0:T(128)} %param.15) | copy-start | bytes 100
  45.3 10.6 %collective-permute-start = (bf16[64,3,2,64]{3,0,2,1:T(8,128)(2,1)S(1)}, bf16[64,3,2,64]{3,0,2,1:T(8,128)(2,1)S(1)}, u32[]{:S(2)}, u32[]{:S(2)}) collective-permute-start(bf16[64,3,2,64]{3,0,2,1:T(8,128)(2,1)S(1)} %get-tuple-element.17), channel_id=1, source_target_pairs={{0,4},{4,8},{8,12},{12,16},{16,20},{20,24},{24,28},{28,0},{1,5},{5... | collective-permute-start | bytes 147464 | tf_op jit(solution)/shard_map/ppermute | solution.py:21
  48.3 7.6 %collective-permute-start.1 = (bf16[64,3,2,64]{3,0,2,1:T(8,128)(2,1)S(1)}, bf16[64,3,2,64]{3,0,2,1:T(8,128)(2,1)S(1)}, u32[]{:S(2)}, u32[]{:S(2)}) collective-permute-start(bf16[64,3,2,64]{3,0,2,1:T(8,128)(2,1)S(1)} %get-tuple-element.18), channel_id=1, source_target_pairs={{4,0},{8,4},{12,8},{16,12},{20,16},{24,20},{28,24},{0,28},{5,1},{9... | collective-permute-start | bytes 147464 | tf_op jit(solution)/shard_map/ppermute | solution.py:22
  56.8 1.0 copy-start.6
  56.8 1.1 copy-start.7
  59.5 19.2 %copy-start.5 = (bf16[2,256,2,256,1]{3,1,0,2,4:T(8,128)(2,1)S(1)}, bf16[2,256,2,256,1]{3,1,0,2,4:T(8,128)(2,1)}, u32[]{:S(2)}) copy-start(bf16[2,256,2,256,1]{3,1,0,2,4:T(8,128)(2,1)} %constant.86) | copy-start | bytes 1572868
  64.2 8.4 %collective-permute-start.2 = (bf16[64,3,2,256]{3,0,2,1:T(8,128)(2,1)S(1)}, bf16[64,3,2,256]{3,0,2,1:T(8,128)(2,1)S(1)}, u32[]{:S(2)}, u32[]{:S(2)}) collective-permute-start(bf16[64,3,2,256]{3,0,2,1:T(8,128)(2,1)S(1)} %copy.130), channel_id=1, source_target_pairs={{4,0},{8,4},{12,8},{16,12},{20,16},{24,20},{28,24},{0,28},{5,1},{9... | collective-permute-start | bytes 589832 | tf_op jit(solution)/shard_map/ppermute | solution.py:30
  67.3 12.7 %copy-start.4 = (bf16[2,256,2,256,1]{3,1,2,0,4:T(8,128)(2,1)S(1)}, bf16[2,256,2,256,1]{3,1,2,0,4:T(8,128)(2,1)}, u32[]{:S(2)}) copy-start(bf16[2,256,2,256,1]{3,1,2,0,4:T(8,128)(2,1)} %constant.88) | copy-start | bytes 1572868
  67.3 9.3 %collective-permute-start.3 = (bf16[64,3,2,256]{3,0,2,1:T(8,128)(2,1)S(1)}, bf16[64,3,2,256]{3,0,2,1:T(8,128)(2,1)S(1)}, u32[]{:S(2)}, u32[]{:S(2)}) collective-permute-start(bf16[64,3,2,256]{3,0,2,1:T(8,128)(2,1)S(1)} %copy.129), channel_id=1, source_target_pairs={{8,0},{12,4},{16,8},{20,12},{24,16},{28,20},{0,24},{4,28},{9,1},{1... | collective-permute-start | bytes 589832 | tf_op jit(solution)/shard_map/ppermute | solution.py:30
  67.4 11.3 %collective-permute-start.4 = (bf16[64,3,2,256]{3,0,2,1:T(8,128)(2,1)S(1)}, bf16[64,3,2,256]{3,0,2,1:T(8,128)(2,1)S(1)}, u32[]{:S(2)}, u32[]{:S(2)}) collective-permute-start(bf16[64,3,2,256]{3,0,2,1:T(8,128)(2,1)S(1)} %copy.128), channel_id=1, source_target_pairs={{12,0},{16,4},{20,8},{24,12},{28,16},{0,20},{4,24},{8,28},{13,1},{... | collective-permute-start | bytes 589832 | tf_op jit(solution)/shard_map/ppermute | solution.py:30
  80.4 15.3 %collective-permute-start.5 = (bf16[64,3,2,256]{3,0,2,1:T(8,128)(2,1)S(1)}, bf16[64,3,2,256]{3,0,2,1:T(8,128)(2,1)}, u32[]{:S(2)}, u32[]{:S(2)}) collective-permute-start(bf16[64,3,2,256]{3,0,2,1:T(8,128)(2,1)S(1)} %fusion.17), channel_id=1, source_target_pairs={{28,0},{0,4},{4,8},{8,12},{12,16},{16,20},{20,24},{24,28},{29,1},{... | collective-permute-start | bytes 589832 | tf_op jit(solution)/shard_map/ppermute | solution.py:30
  86.1 13.3 %collective-permute-start.6 = (bf16[64,3,2,256]{3,0,2,1:T(8,128)(2,1)S(1)}, bf16[64,3,2,256]{3,0,2,1:T(8,128)(2,1)}, u32[]{:S(2)}, u32[]{:S(2)}) collective-permute-start(bf16[64,3,2,256]{3,0,2,1:T(8,128)(2,1)S(1)} %fusion.17), channel_id=1, source_target_pairs={{24,0},{28,4},{0,8},{4,12},{8,16},{12,20},{16,24},{20,28},{25,1},{... | collective-permute-start | bytes 589832 | tf_op jit(solution)/shard_map/ppermute | solution.py:30
  86.1 21.5 %collective-permute-start.7 = (bf16[64,3,2,256]{3,0,2,1:T(8,128)(2,1)S(1)}, bf16[64,3,2,256]{3,0,2,1:T(8,128)(2,1)}, u32[]{:S(2)}, u32[]{:S(2)}) collective-permute-start(bf16[64,3,2,256]{3,0,2,1:T(8,128)(2,1)S(1)} %fusion.17), channel_id=1, source_target_pairs={{20,0},{24,4},{28,8},{0,12},{4,16},{8,20},{12,24},{16,28},{21,1},{... | collective-permute-start | bytes 589832 | tf_op jit(solution)/shard_map/ppermute | solution.py:30
  104.1 8.2 %copy-start.10 = (f32[512]{0:T(512)S(1)}, f32[512]{0:T(512)}, u32[]{:S(2)}) copy-start(f32[512]{0:T(512)} %fusion.106) | copy-start | bytes 6148
  104.1 8.2 %copy-start.11 = (f32[512]{0:T(512)S(1)}, f32[512]{0:T(512)}, u32[]{:S(2)}) copy-start(f32[512]{0:T(512)} %fusion.107) | copy-start | bytes 6148
  104.1 8.2 %copy-start.12 = (f32[512]{0:T(512)S(1)}, f32[512]{0:T(512)}, u32[]{:S(2)}) copy-start(f32[512]{0:T(512)} %fusion.108) | copy-start | bytes 6148
  104.1 8.2 %copy-start.13 = (f32[512]{0:T(512)S(1)}, f32[512]{0:T(512)}, u32[]{:S(2)}) copy-start(f32[512]{0:T(512)} %fusion.109) | copy-start | bytes 6148
  112.3 6.7 %copy-start.2 = (bf16[3,1,128,256]{3,2,1,0:T(8,128)(2,1)S(1)}, bf16[3,1,128,256]{3,2,1,0:T(8,128)(2,1)}, u32[]{:S(2)}) copy-start(bf16[3,1,128,256]{3,2,1,0:T(8,128)(2,1)} %get-tuple-element.39) | copy-start | bytes 589828
  112.3 6.7 %copy-start.3 = (bf16[3,1,128,256]{3,2,1,0:T(8,128)(2,1)S(1)}, bf16[3,1,128,256]{3,2,1,0:T(8,128)(2,1)}, u32[]{:S(2)}) copy-start(bf16[3,1,128,256]{3,2,1,0:T(8,128)(2,1)} %get-tuple-element.40) | copy-start | bytes 589828
  114.3 7.5 %collective-permute-start.8 = (bf16[64,3,2,64]{3,0,2,1:T(8,128)(2,1)S(1)}, bf16[64,3,2,64]{3,0,2,1:T(8,128)(2,1)S(1)}, u32[]{:S(2)}, u32[]{:S(2)}) collective-permute-start(bf16[64,3,2,64]{3,0,2,1:T(8,128)(2,1)S(1)} %get-tuple-element.15), channel_id=1, source_target_pairs={{0,4},{4,8},{8,12},{12,16},{16,20},{20,24},{24,28},{28,0},{1,5},{5... | collective-permute-start | bytes 147464 | tf_op jit(solution)/shard_map/ppermute | solution.py:21
  114.3 7.4 %collective-permute-start.9 = (bf16[64,3,2,64]{3,0,2,1:T(8,128)(2,1)S(1)}, bf16[64,3,2,64]{3,0,2,1:T(8,128)(2,1)S(1)}, u32[]{:S(2)}, u32[]{:S(2)}) collective-permute-start(bf16[64,3,2,64]{3,0,2,1:T(8,128)(2,1)S(1)} %get-tuple-element.16), channel_id=1, source_target_pairs={{4,0},{8,4},{12,8},{16,12},{20,16},{24,20},{28,24},{0,28},{5,1},{9... | collective-permute-start | bytes 147464 | tf_op jit(solution)/shard_map/ppermute | solution.py:22
  122.6 1.0 copy-start.8
  122.6 1.1 copy-start.9
  128.3 0.7 copy-start.15
Sparse Core Ops, SparseCore 0:
  8.9 22.3 all-gather.1
  128.5 44.1 all-reduce.6

commit v2 on v1

v2 whole, which is shorter than its diff:
```python
import functools
import math

import jax
import jax.numpy as jnp
import ml_dtypes
import numpy as np
from jax import lax
from jax.experimental import pallas as pl
from jax.experimental.pallas import tpu as pltpu
from jax.sharding import PartitionSpec as P

FREQS = 256
REACH = 64
LANES = 128
SPAN = 4
MESH = pl.DeviceIdType.MESH


def masked(kernel_taps, band_reach):
    distance = jnp.abs(jnp.arange(2 * REACH + 1, dtype=jnp.int32) - REACH)
    keep = distance[None, :] <= band_reach[:, None]
    return jnp.where(keep[:, None, :], kernel_taps, jnp.zeros_like(kernel_taps))


def taper_row(offset, span_width, first, length):
    places = first + jnp.arange(length, dtype=jnp.int32) - offset
    inside = (places >= 0) & (places < span_width)
    places = jnp.where(inside, places, 0)
    span_float = span_width.astype(jnp.float32)
    taper = 0.5 - 0.5 * jnp.cos((places.astype(jnp.float32) + 0.5) * (2.0 * math.pi) / span_float)
    return jnp.where(inside, taper, 0.0) / jnp.sqrt(span_float)


def dft_table(quarters):
    index = np.arange(FREQS)
    phases = (index[:, None] * index[None, :] % FREQS) * (2.0 * np.pi / FREQS)
    cosine, sine = np.cos(phases), np.sin(phases)
    table = np.stack([np.stack([cosine, -sine], axis=1), np.stack([sine, cosine], axis=1)], axis=0)
    table = table.reshape(2, FREQS, 2, quarters, FREQS // quarters).transpose(0, 1, 3, 2, 4)
    return table.reshape(2 * FREQS, 2 * FREQS).astype(ml_dtypes.bfloat16)


def toeplitz_kernel(seq_ref, out_ref):
    for way in range(2):
        for wave in range(seq_ref.shape[1]):
            lay = []
            for part in range(2):
                row = seq_ref[way, wave, part : part + 1, :]
                spread = jnp.broadcast_to(row, (3 * LANES, 4 * LANES))
                turned = pltpu.roll(spread, 320, 1, stride=1, stride_axis=0)
                lay.append(turned[:, :LANES])
            upper = jnp.concatenate([lay[0], lay[1]], axis=1)
            lower = jnp.concatenate([-lay[1], lay[0]], axis=1)
            out_ref[way, wave] = jnp.concatenate([upper, lower], axis=0).astype(jnp.bfloat16)


def toeplitz_tables(kernel_taps, band_reach):
    taps = masked(kernel_taps, band_reach)
    turned = taps[:, :, ::-1]
    conj = taps * jnp.array([1.0, -1.0], jnp.float32)[None, :, None]
    seq = jnp.stack([turned, conj], axis=0)
    seq = jnp.pad(seq, ((0, 0), (0, 0), (0, 0), (0, 4 * LANES - seq.shape[3])))
    waves = taps.shape[0]
    return pl.pallas_call(
        toeplitz_kernel,
        out_shape=jax.ShapeDtypeStruct((2, waves, 6 * LANES, 2 * LANES), jnp.bfloat16),
        in_specs=[pl.BlockSpec(memory_space=pltpu.VMEM)],
        out_specs=pl.BlockSpec(memory_space=pltpu.VMEM),
    )(seq)


def windows(own, left, right):
    stack = []
    for block in range(4):
        row = []
        for part in range(2):
            for near in (block - 1, block, block + 1):
                if near < 0:
                    row.append(left[:, part * LANES : (part + 1) * LANES])
                elif near > 3:
                    row.append(right[:, part * LANES : (part + 1) * LANES])
                else:
                    start = (part * 4 + near) * LANES
                    row.append(own[:, start : start + LANES])
        stack.append(jnp.concatenate(row, axis=1))
    return jnp.concatenate(stack, axis=0)


def fused_kernel(
    az_size, ht_size, x_ref, toep_ref, taper_ref, dft_ref, idft_ref, prop_ref, propt_ref, target_ref,
    out_ref, edges, halo, send_u, recv_u, recv_t, send_g, recv_g, grad, gedges, ghalo,
    sem_hs, sem_hr, sem_us, sem_ur, sem_ts, sem_tr, sem_gs, sem_gr, sem_bs, sem_br,
):
    a = lax.axis_index("az")
    r = lax.axis_index("ht")
    waves, rows, _ = x_ref.shape
    height = rows * ht_size

    def az(distance):
        return lax.rem(a + (distance + az_size), az_size)

    def ht(distance):
        return lax.rem(r + distance, ht_size)

    barrier = pltpu.get_barrier_semaphore()
    count = 0
    for da in range(-(SPAN - 1), SPAN):
        for dq in range(ht_size):
            if da or dq:
                pl.semaphore_signal(barrier, inc=1, device_id=(az(da), ht(dq)), device_id_type=MESH)
                count += 1

    for wave in range(waves):
        for part in range(2):
            lanes = slice(part * LANES, (part + 1) * LANES)
            first = part * 4 * LANES
            edges[0, wave, :, lanes] = x_ref[wave, :, first : first + LANES]
            edges[1, wave, :, lanes] = x_ref[wave, :, first + 3 * LANES : first + 4 * LANES]
    pl.semaphore_wait(barrier, count)

    def remote(src, dst, send, recv, where):
        return pltpu.make_async_remote_copy(
            src_ref=src, dst_ref=dst, send_sem=send, recv_sem=recv, device_id=where, device_id_type=MESH
        )

    halo_copies = [
        remote(edges.at[side], halo.at[side], sem_hs.at[side], sem_hr.at[side], (az(2 * side - 1), r))
        for side in range(2)
    ]
    for copy in halo_copies:
        copy.start()
    target_copies = [
        remote(target_ref.at[ht(d)], recv_t.at[r], sem_ts.at[d], sem_tr.at[d], (a, ht(d)))
        for d in range(1, ht_size)
    ]
    for copy in target_copies:
        copy.start()
    recv_t[r] = target_ref[r]
    for copy in halo_copies:
        copy.wait_recv()

    def taper(back, block):
        return taper_ref[back * 4 + block : back * 4 + block + 1, :]

    def stage_a(wave, carry):
        lhs = windows(x_ref[wave], halo[1, wave], halo[0, wave])
        y = jnp.dot(lhs, toep_ref[0, wave], preferred_element_type=jnp.float32)
        stack = []
        for back in range(SPAN):
            row = []
            for part in range(2):
                lanes = slice(part * LANES, (part + 1) * LANES)
                for half in range(2):
                    near = y[half * rows : (half + 1) * rows, lanes] * taper(back, half)
                    far = y[(half + 2) * rows : (half + 3) * rows, lanes] * taper(back, half + 2)
                    row.append((near + far).astype(jnp.bfloat16))
            stack.append(jnp.concatenate(row, axis=1))
        folded = jnp.concatenate(stack, axis=0)
        u = jnp.dot(folded, dft_ref[...], preferred_element_type=jnp.float32).astype(jnp.bfloat16)
        for back in range(SPAN):
            for q in range(ht_size):
                send_u[wave, back, q] = u[back * rows : (back + 1) * rows, q * LANES : (q + 1) * LANES]
        for back in range(SPAN - 1, -1, -1):
            for d in range(ht_size):
                if back or d:
                    q = ht(d)
                    remote(
                        send_u.at[wave, back, q], recv_u.at[wave, back, r],
                        sem_us.at[wave, back], sem_ur.at[wave, back], (az(-back), q),
                    ).start()
        recv_u[wave, 0, r] = send_u[wave, 0, r]
        return carry

    def await_bytes(ref, sem):
        pltpu.make_async_copy(ref, ref, sem).wait()

    def group(ref, wave, back):
        first = 1 if back == 0 else 0
        return ref.at[wave, back, pl.ds(0, ht_size - first)]

    lane = lax.broadcasted_iota(jnp.int32, (height, LANES), 1)
    sign = jnp.where(lane < LANES // 2, -1.0, 1.0).astype(jnp.float32)

    def stage_b(wave, carry):
        for back in range(SPAN):
            await_bytes(group(recv_u, wave, back), sem_ur.at[wave, back])
        total = recv_u[wave, 0].astype(jnp.float32)
        for back in range(1, SPAN):
            total = total + recv_u[wave, back].astype(jnp.float32)
        u = total.reshape(height, LANES).astype(jnp.bfloat16)
        z = jnp.dot(prop_ref[wave], u, preferred_element_type=jnp.float32)
        v = z[:height] + sign * pltpu.roll(z[height:], LANES // 2, 1)
        squares = v * v
        power = squares + pltpu.roll(squares, LANES // 2, 1)
        misfit = power - recv_t[:, wave].reshape(height, LANES)
        slope = (2.0 * misfit * v).astype(jnp.bfloat16)
        z = jnp.dot(propt_ref[wave], slope, preferred_element_type=jnp.float32)
        g = z[:height] - sign * pltpu.roll(z[height:], LANES // 2, 1)
        send_g[wave] = g.astype(jnp.bfloat16).reshape(ht_size, rows, LANES)
        for back in range(SPAN - 1, -1, -1):
            for d in range(ht_size):
                if back or d:
                    q = ht(d)
                    remote(
                        send_g.at[wave, q], recv_g.at[wave, back, r],
                        sem_gs.at[wave, back], sem_gr.at[wave, back], (az(back), q),
                    ).start()
        recv_g[wave, 0, r] = send_g[wave, r]
        return carry

    def edge_copy(wave, side):
        return remote(
            gedges.at[wave, side], ghalo.at[wave, side], sem_bs.at[wave, side], sem_br.at[wave, side],
            (az(2 * side - 1), r),
        )

    def stage_c(wave, carry):
        for back in range(SPAN):
            await_bytes(group(recv_g, wave, back), sem_gr.at[wave, back])
        stack = []
        for back in range(SPAN):
            stack.append(jnp.concatenate([recv_g[wave, back, q] for q in range(ht_size)], axis=1))
        lhs = jnp.concatenate(stack, axis=0)
        b = jnp.dot(lhs, idft_ref[...], preferred_element_type=jnp.float32)
        for part in range(2):
            for block in range(4):
                start = (part * 2 + block % 2) * LANES
                total = b[:rows, start : start + LANES] * taper(0, block)
                for back in range(1, SPAN):
                    piece = b[back * rows : (back + 1) * rows, start : start + LANES]
                    total = total + piece * taper(back, block)
                total = total.astype(jnp.bfloat16)
                place = (part * 4 + block) * LANES
                grad[wave, :, place : place + LANES] = total
                if block in (0, 3):
                    lanes = slice(part * LANES, (part + 1) * LANES)
                    gedges[wave, block // 3, :, lanes] = total
        for side in range(2):
            edge_copy(wave, side).start()
        return carry

    def stage_d(wave, carry):
        for side in range(2):
            edge_copy(wave, side).wait()
        lhs = windows(grad[wave], ghalo[wave, 1], ghalo[wave, 0])
        y = jnp.dot(lhs, toep_ref[1, wave], preferred_element_type=jnp.float32)
        for block in range(4):
            for part in range(2):
                place = (part * 4 + block) * LANES
                out_ref[wave, :, place : place + LANES] = y[
                    block * rows : (block + 1) * rows, part * LANES : (part + 1) * LANES
                ]
        for back in range(SPAN):
            first = 1 if back == 0 else 0
            await_bytes(group(send_u, wave, back), sem_us.at[wave, back])
            await_bytes(send_g.at[wave, pl.ds(0, ht_size - first)], sem_gs.at[wave, back])
        return carry

    lax.fori_loop(0, waves, stage_a, 0)
    for copy in target_copies:
        copy.wait()
    lax.fori_loop(0, waves, stage_b, 0)
    lax.fori_loop(0, waves, stage_c, 0)
    lax.fori_loop(0, waves, stage_d, 0)
    for copy in halo_copies:
        copy.wait_send()


def on_device(
    object_field, propagator, kernel_taps, band_reach, sector_offset, sector_width, target_index, target_maps,
    *, az_size, ht_size,
):
    rows, waves, parts, length = object_field.shape
    height = propagator.shape[2]
    here = lax.axis_index("az")
    x = object_field.transpose(1, 0, 2, 3).reshape(waves, rows, parts * length)
    toep = toeplitz_tables(kernel_taps, band_reach)
    tapers = []
    for back in range(SPAN):
        sector = jnp.mod(here - back, az_size)
        tapers.append(taper_row(sector_offset[sector], sector_width[sector], back * length, length))
    tapers = jnp.stack(tapers).reshape(SPAN * length // LANES, LANES)
    dft = dft_table(ht_size)
    prop = propagator.reshape(waves, 2 * height, height)
    propt = propagator.transpose(0, 1, 3, 2).reshape(waves, 2 * height, height)
    plane = lax.dynamic_index_in_dim(target_maps, target_index[here], 0, False)
    plane = plane.reshape(rows, waves, ht_size, FREQS // ht_size).transpose(2, 1, 0, 3)
    plane = jnp.concatenate([plane, plane], axis=3)

    bf16, f32 = jnp.bfloat16, jnp.float32
    dma = pltpu.SemaphoreType.DMA
    vmem = pl.BlockSpec(memory_space=pltpu.VMEM)
    out = pl.pallas_call(
        functools.partial(fused_kernel, az_size, ht_size),
        out_shape=jax.ShapeDtypeStruct((waves, rows, parts * length), f32),
        in_specs=[vmem] * 8,
        out_specs=vmem,
        scratch_shapes=[
            pltpu.VMEM((2, waves, rows, 2 * LANES), bf16),
            pltpu.VMEM((2, waves, rows, 2 * LANES), bf16),
            pltpu.VMEM((waves, SPAN, ht_size, rows, LANES), bf16),
            pltpu.VMEM((waves, SPAN, ht_size, rows, LANES), bf16),
            pltpu.VMEM((ht_size, waves, rows, LANES), f32),
            pltpu.VMEM((waves, ht_size, rows, LANES), bf16),
            pltpu.VMEM((waves, SPAN, ht_size, rows, LANES), bf16),
            pltpu.VMEM((waves, rows, parts * length), bf16),
            pltpu.VMEM((waves, 2, rows, 2 * LANES), bf16),
            pltpu.VMEM((waves, 2, rows, 2 * LANES), bf16),
            dma((2,)), dma((2,)),
            dma((waves, SPAN)), dma((waves, SPAN)),
            dma((ht_size,)), dma((ht_size,)),
            dma((waves, SPAN)), dma((waves, SPAN)),
            dma((waves, 2)), dma((waves, 2)),
        ],
        compiler_params=pltpu.CompilerParams(
            collective_id=0, has_side_effects=True, vmem_limit_bytes=40 * 1024 * 1024
        ),
    )(x, toep, tapers, jnp.asarray(dft), jnp.asarray(np.ascontiguousarray(dft.T)), prop, propt, plane)
    return out.reshape(waves, rows, parts, length).transpose(1, 0, 2, 3)


def solution(mesh):
    in_specs = (P("ht", None, None, "az"), P(), P(), P(), P(), P(), P(), P(None, "ht", None, None))
    out_specs = P("ht", None, None, "az")
    body = functools.partial(on_device, az_size=mesh.shape["az"], ht_size=mesh.shape["ht"])
    return jax.shard_map(body, mesh=mesh, in_specs=in_specs, out_specs=out_specs, check_vma=False)
```

time: 183 us -> 78.2 us (0.43)
  waiting for transfers between devices: 65.1 us -> 0 us
  Pallas kernels: 0 us -> 53.9 us
  other arithmetic: 38.8 us -> 7.67 us
  local copies, waits for them, and re-layouts: 34.6 us -> 11.5 us
  starting transfers between devices: 20 us -> 0 us
  between operations: 19.3 us -> 4.67 us
  matrix products: 3.81 us -> 0 us
    pallas_call x0 -> x2, Pallas kernels: none -> 53.9 us  [the longest x1 51 us: on_device(): pl.pallas_call(functools.partial(fused_kernel, az_size, ht_size), out_sha...]
    unnamed x3 -> x0, waiting for transfers between devices: 42.5 us -> none
    ppermute x10 -> x0, waiting for transfers between devices: 22.6 us -> none  [the longest x6 20.9 us: from_behind(): return lax.ppermute(block, axis, route)]
    ppermute x10 -> x0, starting transfers between devices: 20 us -> none  [the longest x6 8.92 us: from_behind(): return lax.ppermute(block, axis, route)]
    another operation x10 -> x1, local copies, waits for them, and re-layouts: 14.8 us -> 0.07 us  [toeplitz_tables(): seq = jnp.stack([turned, conj], axis=0)]
    and x8 -> x0, other arithmetic: 11 us -> none  [taper_row(): inside = (places >= 0) & (places < span_width)]
    mul x9 -> x0, other arithmetic: 10.9 us -> none  [the longest x8 9.91 us: taper_row(): (places.astype(jnp.float32) + 0.5) * (2.0 * math.pi) / span_float]
    convert_element_type x5 -> x0, local copies, waits for them, and re-layouts: 4.75 us -> none  [the longest x1 3.1 us: on_device(): return lax.psum_scatter(jnp.einsum('wdhcg,hwda->gwca', columns, field_gra...]
  transfers between devices with their start and end apart: 12 -> 0, of which waited for: 7 -> 0; matrix products, arithmetic and copies ran while one was open for 26% -> 0% of each run, Pallas kernels for 0% -> 0%
where the time goes in v2:
time: 78.2 us; the launch traced here: 77.7 us
  Pallas kernels  53.9 us (69%)
  local copies, waits for them, and re-layouts  11.5 us (15%)
  other arithmetic  7.67 us (10%)
  between operations  4.67 us (6%)
    pallas_call x1, Pallas kernels, on_device(): pl.pallas_call(functools.partial(fused_kernel, az_size, ht_size), out_sha...  51 us
    div x4, other arithmetic, taper_row(): return jnp.where(inside, taper, 0.0) / jnp.sqrt(span_float)  5.36 us
    unnamed x15, local copies, waits for them, and re-layouts  4.94 us
    pallas_call x1, Pallas kernels, toeplitz_tables(): pl.pallas_call(toeplitz_kernel, out_shape=jax.ShapeDtypeStruct((2, waves,...  2.83 us
    reshape x2, local copies, waits for them, and re-layouts, on_device(): return out.reshape(waves, rows, parts, length).transpose(1, 0, 2, 3)  1.81 us

profile of v2, /device:TPU:0, one launch (start us, length us, event | category | flops | bytes accessed | tf_op | source)
XLA Modules:
  0.0 77.7 jit_solution(16892180093233826816)
XLA Ops:
  0.0 0.0 copy-start
  0.0 0.0 copy-start.2
  0.0 0.0 copy-start.6
  0.0 1.4 %dynamic_slice.39 = s32[1]{0:T(128)} dynamic-slice(s32[8]{0:T(128)} %param.17, s32[]{:T(128)S(6)} %select_n.145), dynamic_slice_sizes={1} | dynamic-slice | bytes 12 | tf_op jit(solution)/shard_map/dynamic_slice | solution.py:287
  3.3 0.7 broadcast_compare_fusion
  4.1 1.5 %fusion = (s32[1]{0:T(128)}, s32[1]{0:T(128)}, s32[1]{0:T(128)}, s32[1]{0:T(128)}, s32[1]{0:T(128)}, /*index=5*/s32[1]{0:T(128)}, s32[1]{0:T(128)}, s32[1]{0:T(128)}) fusion(s32[8]{0:T(128)} %param.15, s32[]{:T(128)S(6)} %select_n.130, s32[]{:T(128)S(6)} %select_n.134, s32[]{:T(128)S(6)} %select_n.142, s32[]{:T(128)S(6)} %select_n.138, s32[8]{0:T(128)} %param.16), kind=kLoop, calls=%fused_computation.18 | loop fusion | bytes 80 | tf_op jit(solution)/shard_map/dynamic_slice | solution.py:282
  8.2 1.4 %select_divide_fusion.3 = f32[1,512]{1,0:T(1,128)S(1)} fusion(f32[]{:T(128)S(6)} %sqrt.12, f32[]{:T(128)S(6)} %convert_element_type.55, s32[]{:T(128)} %bitcast.4, s32[]{:T(128)} %bitcast.3), kind=kLoop, calls=%fused_computation.14 | loop fusion | flops 6656 | bytes 2064 | tf_op jit(solution)/shard_map/div | solution.py:32
  9.5 1.3 %select_divide_fusion.2 = f32[1,512]{1,0:T(1,128)S(1)} fusion(f32[]{:T(128)S(6)} %sqrt.13, f32[]{:T(128)S(6)} %convert_element_type.57, s32[]{:T(128)} %bitcast.6, s32[]{:T(128)} %bitcast.5), kind=kLoop, calls=%fused_computation.13 | loop fusion | flops 7168 | bytes 2064 | tf_op jit(solution)/shard_map/div | solution.py:32
  10.9 1.3 %select_divide_fusion = f32[1,512]{1,0:T(1,128)S(1)} fusion(f32[]{:T(128)S(6)} %sqrt.15, f32[]{:T(128)S(6)} %convert_element_type.61, s32[]{:T(128)} %bitcast.10, s32[]{:T(128)} %bitcast.9), kind=kLoop, calls=%fused_computation.11 | loop fusion | flops 7168 | bytes 2064 | tf_op jit(solution)/shard_map/div | solution.py:32
  12.2 1.3 %select_divide_fusion.1 = f32[1,512]{1,0:T(1,128)S(1)} fusion(f32[]{:T(128)S(6)} %sqrt.14, f32[]{:T(128)S(6)} %convert_element_type.59, s32[]{:T(128)} %bitcast.8, s32[]{:T(128)} %bitcast.7), kind=kLoop, calls=%fused_computation.12 | loop fusion | flops 7168 | bytes 2064 | tf_op jit(solution)/shard_map/div | solution.py:32
  13.6 0.8 %multiply_bitcast_fusion = (f32[1,3,2,129]{3,2,1,0:T(2,128)S(1)}, f32[3,2,129]{2,1,0:T(2,128)S(1)}) fusion(f32[2]{0:T(128)} %constant.70.clone, f32[3,2,129]{2,1,0:T(2,128)} %param.13, pred[3,129]{1,0:T(4,128)(4,1)S(1)} %broadcast_compare_fusion), kind=kLoop, calls=%fused_computation.9 | loop fusion | flops 1548 | bytes 9683 | tf_op jit(solution)/shard_map/stack | solution.py:62
  14.4 0.2 reverse
  14.5 0.1 slice_bitcast_fusion
  14.6 0.6 select_maximum_fusion.seq_ref
  15.2 0.0 copy-done
  15.3 0.2 reshape.245
  15.5 0.2 pad_maximum_fusion.target_ref
  15.7 0.0 copy-done.6
  15.7 0.3 copy.15
  16.0 1.0 %reshape.241.x_ref = bf16[3,64,1024]{2,1,0:T(8,128)(2,1)} reshape(bf16[3,64,2,512]{3,2,1,0:T(2,128)(2,1)S(1)} %copy.15) | data formatting | bytes 786432 | tf_op jit(solution)/shard_map/reshape | solution.py:277
  17.0 0.0 copy-done.2
  17.0 0.3 copy.16
  17.3 2.8 %shard_map.109.toep_ref = bf16[2,3,768,256]{3,2,1,0:T(8,128)(2,1)} custom-call(f32[2,3,2,512]{3,2,1,0:T(2,128)} %select_maximum_fusion.seq_ref), custom_call_target="tpu_custom_call" | custom-call | tf_op jit(solution)/shard_map/pallas_call | solution.py:65
  20.1 0.0 copy-start.1
  20.1 1.7 %copy-done.1 = bf16[2,3,768,256]{3,2,1,0:T(8,128)(2,1)S(1)} copy-done((bf16[2,3,768,256]{3,2,1,0:T(8,128)(2,1)S(1)}, bf16[2,3,768,256]{3,2,1,0:T(8,128)(2,1)}, u32[]{:S(2)}) %copy-start.1) | copy-done | bytes 2359320
  21.8 0.0 copy-start.3
  21.8 1.0 %copy-done.3 = bf16[3,64,1024]{2,1,0:T(8,128)(2,1)S(1)} copy-done((bf16[3,64,1024]{2,1,0:T(8,128)(2,1)S(1)}, bf16[3,64,1024]{2,1,0:T(8,128)(2,1)}, u32[]{:S(2)}) %copy-start.3) | copy-done | bytes 393240
  22.7 0.0 copy-start.4
  22.8 1.0 %copy-done.4 = bf16[512,512]{1,0:T(8,128)(2,1)S(1)} copy-done((bf16[512,512]{1,0:T(8,128)(2,1)S(1)}, bf16[512,512]{1,0:T(8,128)(2,1)}, u32[]{:S(2)}) %copy-start.4) | copy-done | bytes 524312
  23.8 0.0 copy-start.5
  23.8 1.0 %copy-done.5 = bf16[512,512]{1,0:T(8,128)(2,1)S(1)} copy-done((bf16[512,512]{1,0:T(8,128)(2,1)S(1)}, bf16[512,512]{1,0:T(8,128)(2,1)}, u32[]{:S(2)}) %copy-start.5) | copy-done | bytes 524312
  24.8 51.0 %shard_map.110 = f32[3,64,1024]{2,1,0:T(8,128)S(1)} custom-call(bf16[3,64,1024]{2,1,0:T(8,128)(2,1)S(1)} %copy-done.3, bf16[2,3,768,256]{3,2,1,0:T(8,128)(2,1)S(1)} %copy-done.1, f32[16,128]{1,0:T(8,128)S(1)} %reshape.242.taper_ref, bf16[512,512]{1,0:T(8,128)(2,1)S(1)} %copy-done.5, bf16[512,512]{1,0:T(8,128)(2,1)S(1)} %copy-done.4, ...), custom_call_target="tpu_custom_call" | custom-call | tf_op jit(solution)/shard_map/pallas_call | solution.py:294
  75.9 0.7 reshape.246
  76.6 1.1 %copy.21 = f32[3,64,2,512]{3,2,0,1:T(2,128)} copy(f32[3,64,2,512]{3,2,1,0:T(2,128)S(1)} %reshape.246) | data formatting | bytes 1572864 | tf_op jit(solution)/shard_map/reshape | solution.py:320
  (5 shorter events, 0.1 us)
Async XLA Ops:
  0.0 15.2 %copy-start = (f32[4,64,3,256]{3,1,2,0:T(8,128)S(1)}, f32[4,64,3,256]{3,1,2,0:T(8,128)}, u32[]{:S(2)}) copy-start(f32[4,64,3,256]{3,1,2,0:T(8,128)} %param.18) | copy-start | bytes 2359300
  0.0 17.0 %copy-start.2 = (bf16[3,2,256,256]{3,2,1,0:T(8,128)(2,1)S(1)}, bf16[3,2,256,256]{3,2,1,0:T(8,128)(2,1)}, u32[]{:S(2)}) copy-start(bf16[3,2,256,256]{3,2,1,0:T(8,128)(2,1)} %param.12) | copy-start | bytes 2359300
  0.0 15.7 %copy-start.6 = (bf16[64,3,2,512]{3,2,1,0:T(2,128)(2,1)S(1)}, bf16[64,3,2,512]{3,2,1,0:T(2,128)(2,1)}, u32[]{:S(2)}) copy-start(bf16[64,3,2,512]{3,2,1,0:T(2,128)(2,1)} %param.11) | copy-start | bytes 1179652
  20.1 1.7 %copy-start.1 = (bf16[2,3,768,256]{3,2,1,0:T(8,128)(2,1)S(1)}, bf16[2,3,768,256]{3,2,1,0:T(8,128)(2,1)}, u32[]{:S(2)}) copy-start(bf16[2,3,768,256]{3,2,1,0:T(8,128)(2,1)} %shard_map.109.toep_ref) | copy-start | bytes 7077892
  21.8 1.0 %copy-start.3 = (bf16[3,64,1024]{2,1,0:T(8,128)(2,1)S(1)}, bf16[3,64,1024]{2,1,0:T(8,128)(2,1)}, u32[]{:S(2)}) copy-start(bf16[3,64,1024]{2,1,0:T(8,128)(2,1)} %reshape.241.x_ref) | copy-start | bytes 1179652
  22.7 1.0 %copy-start.4 = (bf16[512,512]{1,0:T(8,128)(2,1)S(1)}, bf16[512,512]{1,0:T(8,128)(2,1)}, u32[]{:S(2)}) copy-start(bf16[512,512]{1,0:T(8,128)(2,1)} %constant.72.clone.idft_ref) | copy-start | bytes 1572868
  23.8 1.0 %copy-start.5 = (bf16[512,512]{1,0:T(8,128)(2,1)S(1)}, bf16[512,512]{1,0:T(8,128)(2,1)}, u32[]{:S(2)}) copy-start(bf16[512,512]{1,0:T(8,128)(2,1)} %constant.71.clone.dft_ref) | copy-start | bytes 1572868

commit v3 on v2

--- a/solution.py
+++ b/solution.py
@@ -15,21 +15,7 @@
 LANES = 128
 SPAN = 4
 MESH = pl.DeviceIdType.MESH
-
-
-def masked(kernel_taps, band_reach):
-    distance = jnp.abs(jnp.arange(2 * REACH + 1, dtype=jnp.int32) - REACH)
-    keep = distance[None, :] <= band_reach[:, None]
-    return jnp.where(keep[:, None, :], kernel_taps, jnp.zeros_like(kernel_taps))
-
-
-def taper_row(offset, span_width, first, length):
-    places = first + jnp.arange(length, dtype=jnp.int32) - offset
-    inside = (places >= 0) & (places < span_width)
-    places = jnp.where(inside, places, 0)
-    span_float = span_width.astype(jnp.float32)
-    taper = 0.5 - 0.5 * jnp.cos((places.astype(jnp.float32) + 0.5) * (2.0 * math.pi) / span_float)
-    return jnp.where(inside, taper, 0.0) / jnp.sqrt(span_float)
+ROWS_BY_ROWS = (((1,), (1,)), ((), ()))
 
 
 def dft_table(quarters):
@@ -41,33 +27,14 @@
     return table.reshape(2 * FREQS, 2 * FREQS).astype(ml_dtypes.bfloat16)
 
 
-def toeplitz_kernel(seq_ref, out_ref):
-    for way in range(2):
-        for wave in range(seq_ref.shape[1]):
-            lay = []
-            for part in range(2):
-                row = seq_ref[way, wave, part : part + 1, :]
-                spread = jnp.broadcast_to(row, (3 * LANES, 4 * LANES))
-                turned = pltpu.roll(spread, 320, 1, stride=1, stride_axis=0)
-                lay.append(turned[:, :LANES])
-            upper = jnp.concatenate([lay[0], lay[1]], axis=1)
-            lower = jnp.concatenate([-lay[1], lay[0]], axis=1)
-            out_ref[way, wave] = jnp.concatenate([upper, lower], axis=0).astype(jnp.bfloat16)
-
-
-def toeplitz_tables(kernel_taps, band_reach):
-    taps = masked(kernel_taps, band_reach)
-    turned = taps[:, :, ::-1]
-    conj = taps * jnp.array([1.0, -1.0], jnp.float32)[None, :, None]
-    seq = jnp.stack([turned, conj], axis=0)
-    seq = jnp.pad(seq, ((0, 0), (0, 0), (0, 0), (0, 4 * LANES - seq.shape[3])))
-    waves = taps.shape[0]
-    return pl.pallas_call(
-        toeplitz_kernel,
-        out_shape=jax.ShapeDtypeStruct((2, waves, 6 * LANES, 2 * LANES), jnp.bfloat16),
-        in_specs=[pl.BlockSpec(memory_space=pltpu.VMEM)],
-        out_specs=pl.BlockSpec(memory_space=pltpu.VMEM),
-    )(seq)
+def forward_toeplitz(row):
+    spread = jnp.broadcast_to(row, (LANES, 4 * LANES))
+    return pltpu.roll(spread, REACH, 1, stride=1, stride_axis=0)[:, : 3 * LANES]
+
+
+def backward_toeplitz(row):
+    spread = jnp.broadcast_to(row, (3 * LANES, 4 * LANES))
+    return pltpu.roll(spread, 5 * REACH, 1, stride=1, stride_axis=0)[:, :LANES]
 
 
 def windows(own, left, right):
@@ -88,9 +55,9 @@
 
 
 def fused_kernel(
-    az_size, ht_size, x_ref, toep_ref, taper_ref, dft_ref, idft_ref, prop_ref, propt_ref, target_ref,
-    out_ref, edges, halo, send_u, recv_u, recv_t, send_g, recv_g, grad, gedges, ghalo,
-    sem_hs, sem_hr, sem_us, sem_ur, sem_ts, sem_tr, sem_gs, sem_gr, sem_bs, sem_br,
+    az_size, ht_size, x_ref, taps_ref, reach_ref, offset_ref, width_ref, dft_hbm, prop_hbm, propt_hbm,
+    target_ref, out_ref, dft_ref, prop_ref, propt_ref, taper_ref, padded, front, behind, edges, halo, send_u, recv_u, recv_t, send_g, recv_g, grad, gedges, ghalo,
+    sem_hs, sem_hr, sem_us, sem_ur, sem_ts, sem_tr, sem_gs, sem_gr, sem_bs, sem_br, sem_in,
 ):
     a = lax.axis_index("az")
     r = lax.axis_index("ht")
@@ -102,6 +69,13 @@
 
     def ht(distance):
         return lax.rem(r + distance, ht_size)
+
+    loads = [
+        pltpu.make_async_copy(src, dst, sem_in.at[i])
+        for i, (src, dst) in enumerate(((dft_hbm, dft_ref), (prop_hbm, prop_ref), (propt_hbm, propt_ref)))
+    ]
+    for load in loads:
+        load.start()
 
     barrier = pltpu.get_barrier_semaphore()
     count = 0
@@ -137,6 +111,31 @@
     for copy in target_copies:
         copy.start()
     recv_t[r] = target_ref[r]
+
+    blocks = lax.broadcasted_iota(jnp.int32, (4, LANES), 0) * LANES
+    spots = blocks + lax.broadcasted_iota(jnp.int32, (4, LANES), 1)
+    for back in range(SPAN):
+        width = width_ref[az(-back)]
+        places = spots + (4 * back * LANES - offset_ref[az(-back)])
+        inside = (places >= 0) & (places < width)
+        places = jnp.where(inside, places, 0).astype(jnp.float32)
+        span = jnp.full((4, LANES), width, jnp.int32).astype(jnp.float32)
+        taper = 0.5 - 0.5 * jnp.cos((places + 0.5) * (2.0 * math.pi) / span)
+        taper_ref[4 * back : 4 * back + 4, :] = jnp.where(inside, taper, 0.0) / jnp.sqrt(span)
+
+    taps_count = 2 * REACH + 1
+    distance = jnp.abs(lax.broadcasted_iota(jnp.int32, (2, 4 * LANES), 1) - REACH)
+    padded[...] = jnp.zeros_like(padded)
+    for wave in range(waves):
+        padded[wave, :, :taps_count] = taps_ref[wave]
+        rows_of = jnp.where(distance <= reach_ref[wave], padded[wave], 0.0)
+        padded[wave] = rows_of
+        real = forward_toeplitz(rows_of[0:1])
+        imag = forward_toeplitz(rows_of[1:2])
+        front[wave, :LANES] = jnp.concatenate([real, -imag], axis=1).astype(jnp.bfloat16)
+        front[wave, LANES:] = jnp.concatenate([imag, real], axis=1).astype(jnp.bfloat16)
+
+    loads[0].wait()
     for copy in halo_copies:
         copy.wait_recv()
 
@@ -145,7 +144,7 @@
 
     def stage_a(wave, carry):
         lhs = windows(x_ref[wave], halo[1, wave], halo[0, wave])
-        y = jnp.dot(lhs, toep_ref[0, wave], preferred_element_type=jnp.float32)
+        y = lax.dot_general(lhs, front[wave], ROWS_BY_ROWS, preferred_element_type=jnp.float32)
         stack = []
         for back in range(SPAN):
             row = []
@@ -222,7 +221,7 @@
         for back in range(SPAN):
             stack.append(jnp.concatenate([recv_g[wave, back, q] for q in range(ht_size)], axis=1))
         lhs = jnp.concatenate(stack, axis=0)
-        b = jnp.dot(lhs, idft_ref[...], preferred_element_type=jnp.float32)
+        b = lax.dot_general(lhs, dft_ref[...], ROWS_BY_ROWS, preferred_element_type=jnp.float32)
         for part in range(2):
             for block in range(4):
                 start = (part * 2 + block % 2) * LANES
@@ -244,7 +243,7 @@
         for side in range(2):
             edge_copy(wave, side).wait()
         lhs = windows(grad[wave], ghalo[wave, 1], ghalo[wave, 0])
-        y = jnp.dot(lhs, toep_ref[1, wave], preferred_element_type=jnp.float32)
+        y = jnp.dot(lhs, behind[wave], preferred_element_type=jnp.float32)
         for block in range(4):
             for part in range(2):
                 place = (part * 4 + block) * LANES
@@ -258,6 +257,13 @@
         return carry
 
     lax.fori_loop(0, waves, stage_a, 0)
+    for wave in range(waves):
+        real = backward_toeplitz(padded[wave, 0:1, :])
+        imag = backward_toeplitz(padded[wave, 1:2, :])
+        behind[wave, : 3 * LANES] = jnp.concatenate([real, -imag], axis=1).astype(jnp.bfloat16)
+        behind[wave, 3 * LANES :] = jnp.concatenate([imag, real], axis=1).astype(jnp.bfloat16)
+    for load in loads[1:]:
+        load.wait()
     for copy in target_copies:
         copy.wait()
     lax.fori_loop(0, waves, stage_b, 0)
@@ -275,13 +281,7 @@
     height = propagator.shape[2]
     here = lax.axis_index("az")
     x = object_field.transpose(1, 0, 2, 3).reshape(waves, rows, parts * length)
-    toep = toeplitz_tables(kernel_taps, band_reach)
-    tapers = []
-    for back in range(SPAN):
-        sector = jnp.mod(here - back, az_size)
-        tapers.append(taper_row(sector_offset[sector], sector_width[sector], back * length, length))
-    tapers = jnp.stack(tapers).reshape(SPAN * length // LANES, LANES)
-    dft = dft_table(ht_size)
+    dft = jnp.asarray(dft_table(ht_size))
     prop = propagator.reshape(waves, 2 * height, height)
     propt = propagator.transpose(0, 1, 3, 2).reshape(waves, 2 * height, height)
     plane = lax.dynamic_index_in_dim(target_maps, target_index[here], 0, False)
@@ -291,12 +291,21 @@
     bf16, f32 = jnp.bfloat16, jnp.float32
     dma = pltpu.SemaphoreType.DMA
     vmem = pl.BlockSpec(memory_space=pltpu.VMEM)
+    smem = pl.BlockSpec(memory_space=pltpu.SMEM)
+    hbm = pl.BlockSpec(memory_space=pltpu.HBM)
     out = pl.pallas_call(
         functools.partial(fused_kernel, az_size, ht_size),
         out_shape=jax.ShapeDtypeStruct((waves, rows, parts * length), f32),
-        in_specs=[vmem] * 8,
+        in_specs=[vmem, vmem, smem, smem, smem, hbm, hbm, hbm, vmem],
         out_specs=vmem,
         scratch_shapes=[
+            pltpu.VMEM(dft.shape, bf16),
+            pltpu.VMEM(prop.shape, bf16),
+            pltpu.VMEM(propt.shape, bf16),
+            pltpu.VMEM((4 * SPAN, LANES), f32),
+            pltpu.VMEM((waves, 2, 4 * LANES), f32),
+            pltpu.VMEM((waves, 2 * LANES, 6 * LANES), bf16),
+            pltpu.VMEM((waves, 6 * LANES, 2 * LANES), bf16),
             pltpu.VMEM((2, waves, rows, 2 * LANES), bf16),
             pltpu.VMEM((2, waves, rows, 2 * LANES), bf16),
             pltpu.VMEM((waves, SPAN, ht_size, rows, LANES), bf16),
@@ -311,12 +320,12 @@
             dma((waves, SPAN)), dma((waves, SPAN)),
             dma((ht_size,)), dma((ht_size,)),
             dma((waves, SPAN)), dma((waves, SPAN)),
-            dma((waves, 2)), dma((waves, 2)),
+            dma((waves, 2)), dma((waves, 2)), dma((3,)),
         ],
         compiler_params=pltpu.CompilerParams(
             collective_id=0, has_side_effects=True, vmem_limit_bytes=40 * 1024 * 1024
         ),
-    )(x, toep, tapers, jnp.asarray(dft), jnp.asarray(np.ascontiguousarray(dft.T)), prop, propt, plane)
+    )(x, kernel_taps, band_reach, sector_offset, sector_width, dft, prop, propt, plane)
     return out.reshape(waves, rows, parts, length).transpose(1, 0, 2, 3)
 
 

time: 78.2 us -> 62.7 us (0.80)
  other arithmetic: 7.67 us -> 0.17 us
  local copies, waits for them, and re-layouts: 11.5 us -> 8.45 us
  between operations: 4.67 us -> 2.04 us
  Pallas kernels: 53.9 us -> 51.7 us
    div x4 -> x0, other arithmetic: 5.36 us -> none  [taper_row(): return jnp.where(inside, taper, 0.0) / jnp.sqrt(span_float)]
    pallas_call x1 -> x0, Pallas kernels: 2.83 us -> none  [toeplitz_tables(): pl.pallas_call(toeplitz_kernel, out_shape=jax.ShapeDtypeStruct((2, waves,...]
    dynamic_slice x1 -> x0, local copies, waits for them, and re-layouts: 1.48 us -> none  [on_device(): sector_offset[sector]]
    another operation x3 -> x0, other arithmetic: 1.41 us -> none  [the longest x2 1.4 us: toeplitz_tables(): seq = jnp.stack([turned, conj], axis=0)]
    dynamic_slice x2, local copies, waits for them, and re-layouts: 1.39 us -> 0.6 us  [on_device(): plane = lax.dynamic_index_in_dim(target_maps, target_index[here], 0, False)]
    unnamed x15 -> x20, local copies, waits for them, and re-layouts: 4.94 us -> 4.26 us
where the time goes in v3:
time: 62.7 us; the launch traced here: 62.4 us
  Pallas kernels  51.7 us (82%)
  local copies, waits for them, and re-layouts  8.45 us (13%)
  between operations  2.04 us (3%)
    pallas_call x1, Pallas kernels, on_device(): pl.pallas_call(functools.partial(fused_kernel, az_size, ht_size), out_sha...  51.7 us
    unnamed x20, local copies, waits for them, and re-layouts  4.26 us
    reshape x2, local copies, waits for them, and re-layouts, on_device(): return out.reshape(waves, rows, parts, length).transpose(1, 0, 2, 3)  1.81 us

profile of v3, /device:TPU:0, one launch (start us, length us, event | category | flops | bytes accessed | tf_op | source)
XLA Modules:
  0.0 62.4 jit_solution(10068349964185721021)
XLA Ops:
  0.0 0.0 copy-start
  0.0 0.0 copy-start.9
  0.0 0.7 %copy-done.9 = s32[8]{0:T(128)S(1)} copy-done((s32[8]{0:T(128)S(1)}, s32[8]{0:T(128)}, u32[]{:S(2)}) %copy-start.9) | copy-done | bytes 56
  0.7 0.6 dynamic_slice.7
  3.3 0.0 copy-done
  3.3 0.2 reshape.19
  3.5 0.0 copy-start.8
  3.5 0.2 pad_maximum_fusion.target_ref
  3.7 0.8 %copy-done.8 = bf16[64,3,2,512]{3,2,1,0:T(2,128)(2,1)S(1)} copy-done((bf16[64,3,2,512]{3,2,1,0:T(2,128)(2,1)S(1)}, bf16[64,3,2,512]{3,2,1,0:T(2,128)(2,1)}, u32[]{:S(2)}) %copy-start.8) | copy-done | bytes 393240
  4.5 0.0 copy-start.1
  4.5 0.3 copy.13
  4.8 1.0 %reshape.16.x_ref = bf16[3,64,1024]{2,1,0:T(8,128)(2,1)} reshape(bf16[3,64,2,512]{3,2,1,0:T(2,128)(2,1)S(1)} %copy.13) | data formatting | bytes 786432 | tf_op jit(solution)/shard_map/reshape | solution.py:283
  5.8 0.0 copy-done.1
  5.8 0.0 copy-start.4
  5.8 0.3 copy.14
  6.1 0.0 copy-start.5
  6.1 0.0 copy-start.6
  6.1 0.0 copy-start.7
  6.1 0.4 copy-done.4
  6.5 0.2 copy-done.5
  6.8 0.0 copy-done.6
  6.8 0.0 copy-done.7
  6.8 0.0 copy-start.2
  6.8 1.0 %copy-done.2 = bf16[3,64,1024]{2,1,0:T(8,128)(2,1)S(1)} copy-done((bf16[3,64,1024]{2,1,0:T(8,128)(2,1)S(1)}, bf16[3,64,1024]{2,1,0:T(8,128)(2,1)}, u32[]{:S(2)}) %copy-start.2) | copy-done | bytes 393240
  7.8 0.0 copy-start.3
  7.8 1.0 %copy-done.3 = bf16[512,512]{1,0:T(8,128)(2,1)S(1)} copy-done((bf16[512,512]{1,0:T(8,128)(2,1)S(1)}, bf16[512,512]{1,0:T(8,128)(2,1)}, u32[]{:S(2)}) %copy-start.3) | copy-done | bytes 524312
  8.8 51.7 %shard_map.91 = f32[3,64,1024]{2,1,0:T(8,128)S(1)} custom-call(bf16[3,64,1024]{2,1,0:T(8,128)(2,1)S(1)} %copy-done.2, f32[3,2,129]{2,1,0:T(2,128)S(1)} %copy-done.4, s32[3]{0:T(128)S(1)} %copy-done.5, s32[8]{0:T(128)S(1)} %copy-done.6, s32[8]{0:T(128)S(1)} %copy-done.7, bf16[512,512]{1,0:T(8,128)(2,1)S(1)} %copy-done.3, bf16[3,512,256]{2,1,0:T(8,128)(2,1)S(1)} %bitcast.16, ...), custom_call_target="tpu_custom_call" | custom-call | tf_op jit(solution)/shard_map/pallas_call | solution.py:296
  60.6 0.7 %reshape.20 = f32[3,64,2,512]{3,2,1,0:T(2,128)S(1)} reshape(f32[3,64,1024]{2,1,0:T(8,128)S(1)} %shard_map.91) | data formatting | bytes 1572864 | tf_op jit(solution)/shard_map/reshape | solution.py:329
  61.2 1.1 %copy.19 = f32[3,64,2,512]{3,2,0,1:T(2,128)} copy(f32[3,64,2,512]{3,2,1,0:T(2,128)S(1)} %reshape.20) | data formatting | bytes 1572864 | tf_op jit(solution)/shard_map/reshape | solution.py:329
  (2 shorter events, 0.1 us)
Async XLA Ops:
  0.0 3.3 %copy-start = (f32[4,64,3,256]{3,1,2,0:T(8,128)S(1)}, f32[4,64,3,256]{3,1,2,0:T(8,128)}, u32[]{:S(2)}) copy-start(f32[4,64,3,256]{3,1,2,0:T(8,128)} %param.16) | copy-start | bytes 2359300
  0.0 0.7 %copy-start.9 = (s32[8]{0:T(128)S(1)}, s32[8]{0:T(128)}, u32[]{:S(2)}) copy-start(s32[8]{0:T(128)} %param.15) | copy-start | bytes 100
  3.5 1.0 %copy-start.8 = (bf16[64,3,2,512]{3,2,1,0:T(2,128)(2,1)S(1)}, bf16[64,3,2,512]{3,2,1,0:T(2,128)(2,1)}, u32[]{:S(2)}) copy-start(bf16[64,3,2,512]{3,2,1,0:T(2,128)(2,1)} %param.9) | copy-start | bytes 1179652
  4.5 1.3 %copy-start.1 = (bf16[3,2,256,256]{3,2,1,0:T(8,128)(2,1)S(1)}, bf16[3,2,256,256]{3,2,1,0:T(8,128)(2,1)}, u32[]{:S(2)}) copy-start(bf16[3,2,256,256]{3,2,1,0:T(8,128)(2,1)} %param.10) | copy-start | bytes 2359300
  5.8 0.7 %copy-start.4 = (f32[3,2,129]{2,1,0:T(2,128)S(1)}, f32[3,2,129]{2,1,0:T(2,128)}, u32[]{:S(2)}) copy-start(f32[3,2,129]{2,1,0:T(2,128)} %taps_ref.1) | copy-start | bytes 9292
  6.1 0.7 %copy-start.5 = (s32[3]{0:T(128)S(1)}, s32[3]{0:T(128)}, u32[]{:S(2)}) copy-start(s32[3]{0:T(128)} %reach_ref.1) | copy-start | bytes 40
  6.1 0.7 %copy-start.6 = (s32[8]{0:T(128)S(1)}, s32[8]{0:T(128)}, u32[]{:S(2)}) copy-start(s32[8]{0:T(128)} %offset_ref.1) | copy-start | bytes 100
  6.1 0.7 %copy-start.7 = (s32[8]{0:T(128)S(1)}, s32[8]{0:T(128)}, u32[]{:S(2)}) copy-start(s32[8]{0:T(128)} %width_ref.1) | copy-start | bytes 100
  6.8 1.0 %copy-start.2 = (bf16[3,64,1024]{2,1,0:T(8,128)(2,1)S(1)}, bf16[3,64,1024]{2,1,0:T(8,128)(2,1)}, u32[]{:S(2)}) copy-start(bf16[3,64,1024]{2,1,0:T(8,128)(2,1)} %reshape.16.x_ref) | copy-start | bytes 1179652
  7.8 1.0 %copy-start.3 = (bf16[512,512]{1,0:T(8,128)(2,1)S(1)}, bf16[512,512]{1,0:T(8,128)(2,1)}, u32[]{:S(2)}) copy-start(bf16[512,512]{1,0:T(8,128)(2,1)} %constant.17.clone.dft_hbm) | copy-start | bytes 1572868

commit v4 on v3

--- a/solution.py
+++ b/solution.py
@@ -55,9 +55,9 @@
 
 
 def fused_kernel(
-    az_size, ht_size, x_ref, taps_ref, reach_ref, offset_ref, width_ref, dft_hbm, prop_hbm, propt_hbm,
-    target_ref, out_ref, dft_ref, prop_ref, propt_ref, taper_ref, padded, front, behind, edges, halo, send_u, recv_u, recv_t, send_g, recv_g, grad, gedges, ghalo,
-    sem_hs, sem_hr, sem_us, sem_ur, sem_ts, sem_tr, sem_gs, sem_gr, sem_bs, sem_br, sem_in,
+    az_size, ht_size, x_hbm, taps_ref, reach_ref, offset_ref, width_ref, dft_hbm, prop_hbm, propt_hbm,
+    target_ref, out_ref, x_ref, dft_ref, prop_ref, propt_ref, taper_ref, padded, front, behind, relay, edges, halo, send_u, recv_u, recv_t, send_g, recv_g, grad, gedges, ghalo,
+    sem_hs, sem_hr, sem_us, sem_ur, sem_ts, sem_tr, sem_gs, sem_gr, sem_bs, sem_br, sem_rs, sem_rr, sem_in,
 ):
     a = lax.axis_index("az")
     r = lax.axis_index("ht")
@@ -70,21 +70,26 @@
     def ht(distance):
         return lax.rem(r + distance, ht_size)
 
+    pairs = (
+        (x_hbm, x_ref), (dft_hbm, dft_ref), (prop_hbm, prop_ref), (propt_hbm, propt_ref),
+        (target_ref.at[r], recv_t.at[r]),
+    )
     loads = [
         pltpu.make_async_copy(src, dst, sem_in.at[i])
-        for i, (src, dst) in enumerate(((dft_hbm, dft_ref), (prop_hbm, prop_ref), (propt_hbm, propt_ref)))
+        for i, (src, dst) in enumerate(pairs)
     ]
     for load in loads:
         load.start()
 
     barrier = pltpu.get_barrier_semaphore()
     count = 0
-    for da in range(-(SPAN - 1), SPAN):
+    for da in range(-2, 3):
         for dq in range(ht_size):
             if da or dq:
                 pl.semaphore_signal(barrier, inc=1, device_id=(az(da), ht(dq)), device_id_type=MESH)
                 count += 1
 
+    loads[0].wait()
     for wave in range(waves):
         for part in range(2):
             lanes = slice(part * LANES, (part + 1) * LANES)
@@ -110,7 +115,6 @@
     ]
     for copy in target_copies:
         copy.start()
-    recv_t[r] = target_ref[r]
 
     blocks = lax.broadcasted_iota(jnp.int32, (4, LANES), 0) * LANES
     spots = blocks + lax.broadcasted_iota(jnp.int32, (4, LANES), 1)
@@ -135,12 +139,24 @@
         front[wave, :LANES] = jnp.concatenate([real, -imag], axis=1).astype(jnp.bfloat16)
         front[wave, LANES:] = jnp.concatenate([imag, real], axis=1).astype(jnp.bfloat16)
 
-    loads[0].wait()
+    loads[1].wait()
     for copy in halo_copies:
         copy.wait_recv()
 
     def taper(back, block):
         return taper_ref[back * 4 + block : back * 4 + block + 1, :]
+
+    def relay_copy(wave):
+        return remote(send_u.at[wave, 3], relay.at[wave], sem_us.at[wave, 3], sem_ur.at[wave, 3], (az(-1), r))
+
+    def spread_u(wave, back):
+        for d in range(ht_size):
+            if back or d:
+                q = ht(d)
+                remote(
+                    send_u.at[wave, back, q], recv_u.at[wave, back, r],
+                    sem_us.at[wave, back], sem_ur.at[wave, back], (az(-back), q),
+                ).start()
 
     def stage_a(wave, carry):
         lhs = windows(x_ref[wave], halo[1, wave], halo[0, wave])
@@ -160,15 +176,17 @@
         for back in range(SPAN):
             for q in range(ht_size):
                 send_u[wave, back, q] = u[back * rows : (back + 1) * rows, q * LANES : (q + 1) * LANES]
-        for back in range(SPAN - 1, -1, -1):
-            for d in range(ht_size):
-                if back or d:
-                    q = ht(d)
-                    remote(
-                        send_u.at[wave, back, q], recv_u.at[wave, back, r],
-                        sem_us.at[wave, back], sem_ur.at[wave, back], (az(-back), q),
-                    ).start()
+        relay_copy(wave).start()
+        spread_u(wave, 1)
+        spread_u(wave, 0)
         recv_u[wave, 0, r] = send_u[wave, 0, r]
+        return carry
+
+    def stage_r(wave, carry):
+        relay_copy(wave).wait_recv()
+        both = send_u[wave, 2].astype(jnp.float32) + relay[wave].astype(jnp.float32)
+        send_u[wave, 2] = both.astype(jnp.bfloat16)
+        spread_u(wave, 2)
         return carry
 
     def await_bytes(ref, sem):
@@ -182,10 +200,10 @@
     sign = jnp.where(lane < LANES // 2, -1.0, 1.0).astype(jnp.float32)
 
     def stage_b(wave, carry):
-        for back in range(SPAN):
+        for back in range(3):
             await_bytes(group(recv_u, wave, back), sem_ur.at[wave, back])
         total = recv_u[wave, 0].astype(jnp.float32)
-        for back in range(1, SPAN):
+        for back in range(1, 3):
             total = total + recv_u[wave, back].astype(jnp.float32)
         u = total.reshape(height, LANES).astype(jnp.bfloat16)
         z = jnp.dot(prop_ref[wave], u, preferred_element_type=jnp.float32)
@@ -197,7 +215,7 @@
         z = jnp.dot(propt_ref[wave], slope, preferred_element_type=jnp.float32)
         g = z[:height] - sign * pltpu.roll(z[height:], LANES // 2, 1)
         send_g[wave] = g.astype(jnp.bfloat16).reshape(ht_size, rows, LANES)
-        for back in range(SPAN - 1, -1, -1):
+        for back in (2, 1, 0):
             for d in range(ht_size):
                 if back or d:
                     q = ht(d)
@@ -208,6 +226,16 @@
         recv_g[wave, 0, r] = send_g[wave, r]
         return carry
 
+    def pass_copy(wave):
+        return remote(
+            recv_g.at[wave, 2], recv_g.at[wave, 3], sem_rs.at[wave], sem_rr.at[wave], (az(1), r)
+        )
+
+    def stage_x(wave, carry):
+        await_bytes(group(recv_g, wave, 2), sem_gr.at[wave, 2])
+        pass_copy(wave).start()
+        return carry
+
     def edge_copy(wave, side):
         return remote(
             gedges.at[wave, side], ghalo.at[wave, side], sem_bs.at[wave, side], sem_br.at[wave, side],
@@ -215,8 +243,9 @@
         )
 
     def stage_c(wave, carry):
-        for back in range(SPAN):
+        for back in range(2):
             await_bytes(group(recv_g, wave, back), sem_gr.at[wave, back])
+        pass_copy(wave).wait_recv()
         stack = []
         for back in range(SPAN):
             stack.append(jnp.concatenate([recv_g[wave, back, q] for q in range(ht_size)], axis=1))
@@ -253,22 +282,35 @@
         for back in range(SPAN):
             first = 1 if back == 0 else 0
             await_bytes(group(send_u, wave, back), sem_us.at[wave, back])
-            await_bytes(send_g.at[wave, pl.ds(0, ht_size - first)], sem_gs.at[wave, back])
-        return carry
-
-    lax.fori_loop(0, waves, stage_a, 0)
+            if back < 3:
+                await_bytes(send_g.at[wave, pl.ds(0, ht_size - first)], sem_gs.at[wave, back])
+        pass_copy(wave).wait_send()
+        return carry
+
+    def ahead(wave, carry):
+        stage_a(wave, 0)
+        lax.cond(wave > 0, lambda: stage_r(wave - 1, 0), lambda: 0)
+        return carry
+
+    def middle(step, carry):
+        lax.cond(step < waves, lambda: stage_b(step, 0), lambda: 0)
+        lax.cond((step > 0) & (step <= waves), lambda: stage_x(step - 1, 0), lambda: 0)
+        lax.cond((step > 1) & (step <= waves + 1), lambda: stage_c(step - 2, 0), lambda: 0)
+        lax.cond(step > 2, lambda: stage_d(step - 3, 0), lambda: 0)
+        return carry
+
+    lax.fori_loop(0, waves, ahead, 0)
+    stage_r(waves - 1, 0)
     for wave in range(waves):
         real = backward_toeplitz(padded[wave, 0:1, :])
         imag = backward_toeplitz(padded[wave, 1:2, :])
         behind[wave, : 3 * LANES] = jnp.concatenate([real, -imag], axis=1).astype(jnp.bfloat16)
         behind[wave, 3 * LANES :] = jnp.concatenate([imag, real], axis=1).astype(jnp.bfloat16)
-    for load in loads[1:]:
+    for load in loads[2:]:
         load.wait()
     for copy in target_copies:
         copy.wait()
-    lax.fori_loop(0, waves, stage_b, 0)
-    lax.fori_loop(0, waves, stage_c, 0)
-    lax.fori_loop(0, waves, stage_d, 0)
+    lax.fori_loop(0, waves + 3, middle, 0)
     for copy in halo_copies:
         copy.wait_send()
 
@@ -296,9 +338,10 @@
     out = pl.pallas_call(
         functools.partial(fused_kernel, az_size, ht_size),
         out_shape=jax.ShapeDtypeStruct((waves, rows, parts * length), f32),
-        in_specs=[vmem, vmem, smem, smem, smem, hbm, hbm, hbm, vmem],
+        in_specs=[hbm, vmem, smem, smem, smem, hbm, hbm, hbm, hbm],
         out_specs=vmem,
         scratch_shapes=[
+            pltpu.VMEM(x.shape, bf16),
             pltpu.VMEM(dft.shape, bf16),
             pltpu.VMEM(prop.shape, bf16),
             pltpu.VMEM(propt.shape, bf16),
@@ -306,6 +349,7 @@
             pltpu.VMEM((waves, 2, 4 * LANES), f32),
             pltpu.VMEM((waves, 2 * LANES, 6 * LANES), bf16),
             pltpu.VMEM((waves, 6 * LANES, 2 * LANES), bf16),
+            pltpu.VMEM((waves, ht_size, rows, LANES), bf16),
             pltpu.VMEM((2, waves, rows, 2 * LANES), bf16),
             pltpu.VMEM((2, waves, rows, 2 * LANES), bf16),
             pltpu.VMEM((waves, SPAN, ht_size, rows, LANES), bf16),
@@ -320,10 +364,10 @@
             dma((waves, SPAN)), dma((waves, SPAN)),
             dma((ht_size,)), dma((ht_size,)),
             dma((waves, SPAN)), dma((waves, SPAN)),
-            dma((waves, 2)), dma((waves, 2)), dma((3,)),
+            dma((waves, 2)), dma((waves, 2)), dma((waves,)), dma((waves,)), dma((5,)),
         ],
         compiler_params=pltpu.CompilerParams(
-            collective_id=0, has_side_effects=True, vmem_limit_bytes=40 * 1024 * 1024
+            collective_id=0, has_side_effects=True, vmem_limit_bytes=60 * 1024 * 1024
         ),
     )(x, kernel_taps, band_reach, sector_offset, sector_width, dft, prop, propt, plane)
     return out.reshape(waves, rows, parts, length).transpose(1, 0, 2, 3)

time: 62.7 us -> 60.8 us (0.970)
  local copies, waits for them, and re-layouts: 8.45 us -> 6.99 us
  Pallas kernels: 51.7 us -> 50.6 us
  other arithmetic: 0.17 us -> 0.94 us
    unnamed x20 -> x8, local copies, waits for them, and re-layouts: 4.26 us -> 0.79 us
    reshape x2, local copies, waits for them, and re-layouts: 1.81 us -> 2.95 us  [on_device(): return out.reshape(waves, rows, parts, length).transpose(1, 0, 2, 3)]
    pallas_call x1, Pallas kernels: 51.7 us -> 50.6 us  [on_device(): pl.pallas_call(functools.partial(fused_kernel, az_size, ht_size), out_sha...]
    transpose x1, local copies, waits for them, and re-layouts: 0.27 us -> 1.15 us  [on_device(): propt = propagator.transpose(0, 1, 3, 2).reshape(waves, 2 * height, height)]
    concatenate x1, other arithmetic: 0.17 us -> 0.94 us  [on_device(): plane = jnp.concatenate([plane, plane], axis=3)]
where the time goes in v4:
time: 60.8 us; the launch traced here: 60.6 us
  Pallas kernels  50.6 us (83%)
  local copies, waits for them, and re-layouts  6.99 us (11%)
  between operations  2 us (3%)
  other arithmetic  0.94 us (2%)
    pallas_call x1, Pallas kernels, on_device(): pl.pallas_call(functools.partial(fused_kernel, az_size, ht_size), out_sha...  50.6 us
    reshape x2, local copies, waits for them, and re-layouts, on_device(): return out.reshape(waves, rows, parts, length).transpose(1, 0, 2, 3)  2.95 us

profile of v4, /device:TPU:0, one launch (start us, length us, event | category | flops | bytes accessed | tf_op | source)
XLA Modules:
  0.0 60.6 jit_solution(17984646235353932706)
XLA Ops:
  0.0 0.0 copy-start
  0.0 0.0 copy-start.3
  0.0 0.7 %copy-done.3 = s32[8]{0:T(128)S(1)} copy-done((s32[8]{0:T(128)S(1)}, s32[8]{0:T(128)}, u32[]{:S(2)}) %copy-start.3) | copy-done | bytes 56
  0.7 0.6 dynamic_slice.7
  3.3 0.0 copy-done
  3.3 0.2 reshape.19
  3.5 0.0 copy-start.2
  3.5 0.9 %pad_maximum_fusion.target_ref = f32[4,3,64,128]{3,2,1,0:T(8,128)} fusion(f32[4,3,64,64]{3,2,1,0:T(8,128)S(1)} %bitcast.18), kind=kLoop, calls=%fused_computation.1 | loop fusion | flops 98304 | bytes 589824 | tf_op jit(solution)/shard_map/concatenate | solution.py:331
  4.5 0.0 copy-done.2
  4.5 0.0 copy-start.1
  4.5 0.3 copy.13
  4.8 1.0 %reshape.16.x_hbm = bf16[3,64,1024]{2,1,0:T(8,128)(2,1)} reshape(bf16[3,64,2,512]{3,2,1,0:T(2,128)(2,1)S(1)} %copy.13) | data formatting | bytes 786432 | tf_op jit(solution)/shard_map/reshape | solution.py:325
  5.8 0.0 copy-done.1
  5.8 1.2 %copy.14 = bf16[3,2,256,256]{3,2,1,0:T(8,128)(2,1)} copy(bf16[3,2,256,256]{2,3,1,0:T(8,128)(2,1)S(1)} %bitcast.16) | data formatting | bytes 1572864 | tf_op jit(solution)/shard_map/transpose | solution.py:328
  7.0 50.6 %shard_map.91 = f32[3,64,1024]{2,1,0:T(8,128)} custom-call(bf16[3,64,1024]{2,1,0:T(8,128)(2,1)} %reshape.16.x_hbm, f32[3,2,129]{2,1,0:T(2,128)} %taps_ref.1, s32[3]{0:T(128)} %reach_ref.1, s32[8]{0:T(128)} %offset_ref.1, s32[8]{0:T(128)} %width_ref.1, bf16[512,512]{1,0:T(8,128)(2,1)} %constant.17.clone.dft_hbm, bf16[3,512,256]{2,1,0:T(8,128)(2,1)} %bitcast.15, ...), custom_call_target="tpu_custom_call" | custom-call | tf_op jit(solution)/shard_map/pallas_call | solution.py:338
  57.6 1.8 %reshape.20 = f32[3,64,2,512]{3,2,1,0:T(2,128)S(1)} reshape(f32[3,64,1024]{2,1,0:T(8,128)} %shard_map.91) | data formatting | bytes 1572864 | tf_op jit(solution)/shard_map/reshape | solution.py:373
  59.4 1.1 %copy.19 = f32[3,64,2,512]{3,2,0,1:T(2,128)} copy(f32[3,64,2,512]{3,2,1,0:T(2,128)S(1)} %reshape.20) | data formatting | bytes 1572864 | tf_op jit(solution)/shard_map/reshape | solution.py:373
  (2 shorter events, 0.1 us)
Async XLA Ops:
  0.0 3.3 %copy-start = (f32[4,64,3,256]{3,1,2,0:T(8,128)S(1)}, f32[4,64,3,256]{3,1,2,0:T(8,128)}, u32[]{:S(2)}) copy-start(f32[4,64,3,256]{3,1,2,0:T(8,128)} %param.16) | copy-start | bytes 2359300
  0.0 0.7 %copy-start.3 = (s32[8]{0:T(128)S(1)}, s32[8]{0:T(128)}, u32[]{:S(2)}) copy-start(s32[8]{0:T(128)} %param.15) | copy-start | bytes 100
  3.5 1.0 %copy-start.2 = (bf16[64,3,2,512]{3,2,1,0:T(2,128)(2,1)S(1)}, bf16[64,3,2,512]{3,2,1,0:T(2,128)(2,1)}, u32[]{:S(2)}) copy-start(bf16[64,3,2,512]{3,2,1,0:T(2,128)(2,1)} %param.9) | copy-start | bytes 1179652
  4.5 1.3 %copy-start.1 = (bf16[3,2,256,256]{3,2,1,0:T(8,128)(2,1)S(1)}, bf16[3,2,256,256]{3,2,1,0:T(8,128)(2,1)}, u32[]{:S(2)}) copy-start(bf16[3,2,256,256]{3,2,1,0:T(8,128)(2,1)} %param.10) | copy-start | bytes 2359300

commit v5 on v4

--- a/solution.py
+++ b/solution.py
@@ -56,7 +56,7 @@
 
 def fused_kernel(
     az_size, ht_size, x_hbm, taps_ref, reach_ref, offset_ref, width_ref, dft_hbm, prop_hbm, propt_hbm,
-    target_ref, out_ref, x_ref, dft_ref, prop_ref, propt_ref, taper_ref, padded, front, behind, relay, edges, halo, send_u, recv_u, recv_t, send_g, recv_g, grad, gedges, ghalo,
+    index_ref, maps_ref, out_ref, target_ref, x_ref, dft_ref, prop_ref, propt_ref, taper_ref, padded, front, behind, relay, edges, halo, send_u, recv_u, recv_t, send_g, recv_g, grad, gedges, ghalo,
     sem_hs, sem_hr, sem_us, sem_ur, sem_ts, sem_tr, sem_gs, sem_gr, sem_bs, sem_br, sem_rs, sem_rr, sem_in,
 ):
     a = lax.axis_index("az")
@@ -72,7 +72,6 @@
 
     pairs = (
         (x_hbm, x_ref), (dft_hbm, dft_ref), (prop_hbm, prop_ref), (propt_hbm, propt_ref),
-        (target_ref.at[r], recv_t.at[r]),
     )
     loads = [
         pltpu.make_async_copy(src, dst, sem_in.at[i])
@@ -109,6 +108,14 @@
     ]
     for copy in halo_copies:
         copy.start()
+    pattern = index_ref[a]
+    half = LANES // 2
+    for wave in range(waves):
+        plane = maps_ref[pattern, wave]
+        for q in range(ht_size):
+            piece = plane[:, q * half : (q + 1) * half]
+            target_ref[q, wave] = jnp.concatenate([piece, piece], axis=1)
+    recv_t[r] = target_ref[r]
     target_copies = [
         remote(target_ref.at[ht(d)], recv_t.at[r], sem_ts.at[d], sem_tr.at[d], (a, ht(d)))
         for d in range(1, ht_size)
@@ -321,14 +328,11 @@
 ):
     rows, waves, parts, length = object_field.shape
     height = propagator.shape[2]
-    here = lax.axis_index("az")
     x = object_field.transpose(1, 0, 2, 3).reshape(waves, rows, parts * length)
     dft = jnp.asarray(dft_table(ht_size))
     prop = propagator.reshape(waves, 2 * height, height)
     propt = propagator.transpose(0, 1, 3, 2).reshape(waves, 2 * height, height)
-    plane = lax.dynamic_index_in_dim(target_maps, target_index[here], 0, False)
-    plane = plane.reshape(rows, waves, ht_size, FREQS // ht_size).transpose(2, 1, 0, 3)
-    plane = jnp.concatenate([plane, plane], axis=3)
+    maps = target_maps.transpose(0, 2, 1, 3)
 
     bf16, f32 = jnp.bfloat16, jnp.float32
     dma = pltpu.SemaphoreType.DMA
@@ -338,9 +342,10 @@
     out = pl.pallas_call(
         functools.partial(fused_kernel, az_size, ht_size),
         out_shape=jax.ShapeDtypeStruct((waves, rows, parts * length), f32),
-        in_specs=[hbm, vmem, smem, smem, smem, hbm, hbm, hbm, hbm],
+        in_specs=[hbm, vmem, smem, smem, smem, hbm, hbm, hbm, smem, vmem],
         out_specs=vmem,
         scratch_shapes=[
+            pltpu.VMEM((ht_size, waves, rows, LANES), f32),
             pltpu.VMEM(x.shape, bf16),
             pltpu.VMEM(dft.shape, bf16),
             pltpu.VMEM(prop.shape, bf16),
@@ -364,12 +369,12 @@
             dma((waves, SPAN)), dma((waves, SPAN)),
             dma((ht_size,)), dma((ht_size,)),
             dma((waves, SPAN)), dma((waves, SPAN)),
-            dma((waves, 2)), dma((waves, 2)), dma((waves,)), dma((waves,)), dma((5,)),
+            dma((waves, 2)), dma((waves, 2)), dma((waves,)), dma((waves,)), dma((4,)),
         ],
         compiler_params=pltpu.CompilerParams(
             collective_id=0, has_side_effects=True, vmem_limit_bytes=60 * 1024 * 1024
         ),
-    )(x, kernel_taps, band_reach, sector_offset, sector_width, dft, prop, propt, plane)
+    )(x, kernel_taps, band_reach, sector_offset, sector_width, dft, prop, propt, target_index, maps)
     return out.reshape(waves, rows, parts, length).transpose(1, 0, 2, 3)
 
 

time: 60.8 us -> 57.6 us (0.947)
  between operations: 2 us -> 0.02 us
  other arithmetic: 0.94 us -> 0 us
    transpose x1, local copies, waits for them, and re-layouts: 0.27 us -> 1.34 us  [on_device(): x = object_field.transpose(1, 0, 2, 3).reshape(waves, rows, parts * length)]
    concatenate x1 -> x0, other arithmetic: 0.94 us -> none  [on_device(): plane = jnp.concatenate([plane, plane], axis=3)]
    unnamed x8 -> x2, local copies, waits for them, and re-layouts: 0.79 us -> 0.01 us
where the time goes in v5:
time: 57.6 us; the launch traced here: 57.4 us
  Pallas kernels  50.9 us (88%)
  local copies, waits for them, and re-layouts  6.45 us (11%)
    pallas_call x1, Pallas kernels, on_device(): pl.pallas_call(functools.partial(fused_kernel, az_size, ht_size), out_sha...  50.9 us
    reshape x2, local copies, waits for them, and re-layouts, on_device(): return out.reshape(waves, rows, parts, length).transpose(1, 0, 2, 3)  2.95 us
    transpose x1, local copies, waits for them, and re-layouts, on_device(): x = object_field.transpose(1, 0, 2, 3).reshape(waves, rows, parts * length)  1.34 us
    transpose x1, local copies, waits for them, and re-layouts, on_device(): propt = propagator.transpose(0, 1, 3, 2).reshape(waves, 2 * height, height)  1.15 us

profile of v5, /device:TPU:0, one launch (start us, length us, event | category | flops | bytes accessed | tf_op | source)
XLA Modules:
  0.0 57.4 jit_solution(7680721238357655840)
XLA Ops:
  0.0 0.0 copy-start
  0.0 1.3 %copy.10 = bf16[3,64,2,512]{3,2,1,0:T(2,128)(2,1)S(1)} copy(bf16[3,64,2,512]{3,2,0,1:T(2,128)(2,1)} %bitcast.12) | data formatting | bytes 786432 | tf_op jit(solution)/shard_map/transpose | solution.py:331
  1.3 1.0 %reshape.12.x_hbm = bf16[3,64,1024]{2,1,0:T(8,128)(2,1)} reshape(bf16[3,64,2,512]{3,2,1,0:T(2,128)(2,1)S(1)} %copy.10) | data formatting | bytes 786432 | tf_op jit(solution)/shard_map/reshape | solution.py:331
  2.4 0.0 copy-done
  2.4 1.2 %copy.11 = bf16[3,2,256,256]{3,2,1,0:T(8,128)(2,1)} copy(bf16[3,2,256,256]{2,3,1,0:T(8,128)(2,1)S(1)} %bitcast.9) | data formatting | bytes 1572864 | tf_op jit(solution)/shard_map/transpose | solution.py:334
  3.5 50.9 %shard_map.91 = f32[3,64,1024]{2,1,0:T(8,128)} custom-call(bf16[3,64,1024]{2,1,0:T(8,128)(2,1)} %reshape.12.x_hbm, f32[3,2,129]{2,1,0:T(2,128)} %taps_ref.1, s32[3]{0:T(128)} %reach_ref.1, s32[8]{0:T(128)} %offset_ref.1, s32[8]{0:T(128)} %width_ref.1, bf16[512,512]{1,0:T(8,128)(2,1)} %constant.2.clone.dft_hbm, bf16[3,512,256]{2,1,0:T(8,128)(2,1)} %bitcast.8, ...), custom_call_target="tpu_custom_call" | custom-call | tf_op jit(solution)/shard_map/pallas_call | solution.py:342
  54.5 1.8 %reshape.15 = f32[3,64,2,512]{3,2,1,0:T(2,128)S(1)} reshape(f32[3,64,1024]{2,1,0:T(8,128)} %shard_map.91) | data formatting | bytes 1572864 | tf_op jit(solution)/shard_map/reshape | solution.py:378
  56.3 1.1 %copy.14 = f32[3,64,2,512]{3,2,0,1:T(2,128)} copy(f32[3,64,2,512]{3,2,1,0:T(2,128)S(1)} %reshape.15) | data formatting | bytes 1572864 | tf_op jit(solution)/shard_map/reshape | solution.py:378
Async XLA Ops:
  0.0 2.4 %copy-start = (bf16[3,2,256,256]{3,2,1,0:T(8,128)(2,1)S(1)}, bf16[3,2,256,256]{3,2,1,0:T(8,128)(2,1)}, u32[]{:S(2)}) copy-start(bf16[3,2,256,256]{3,2,1,0:T(8,128)(2,1)} %param.10) | copy-start | bytes 2359300
